TPU v7x, 32 devices: a whole 2x2x4 slice. The times are simulated.
32 devices in a mesh: seq: 8 (over z, core), head: 4 (over y, x).
Axes of the slice: x: 2, y: 2, z: 4, core: 2. Of those that a mesh axis runs over, the one named last changes fastest.
Arguments:
- queries: bfloat16 [8192, 4096], P('seq', 'head'), may hold values from -6 to 6
- key_rows: bfloat16 [8192, 4096], P('seq', 'head'), may hold values from -6 to 6
- value_rows: bfloat16 [8192, 4096], P('seq', 'head'), may hold values from -6 to 6
- out_weight: bfloat16 [4096, 4096], P('head'), may hold values from -0.375 to 0.375
- cotangent: bfloat16 [8192, 4096], P('seq', 'head'), may hold values from -1.5 to 1.5
- pattern: int32 [64, 6], P('seq'), may hold values 0 or 1
Outputs:
- output: bfloat16 [8192, 4096], P('seq', 'head')
- grad_query: bfloat16 [8192, 4096], P('seq', 'head')
- grad_keys: bfloat16 [8192, 4096], P('seq', 'head')
- grad_values: bfloat16 [8192, 4096], P('seq', 'head')
- grad_weight: float32 [4096, 4096], P('seq', 'head')
All inputs are finite; a program needn't handle non-finite values. No bound on the sum of `pattern` on one device may be relied on, other than what follows from the above.
Results may differ from a plain program's by a relative error of at most 0.0076.
Values may be sent and summed in bfloat16 or wider, within the bound.
A program may use at most 256 MiB of HBM per device.

v0:
```python
import math

import jax
import jax.numpy as jnp
from jax import lax
from jax.sharding import PartitionSpec as P

DH = 128
BLK = 128


LOG_TWO = math.log(2.0)


def swapped(value, axis, bit):
    mask = 2**bit
    pairs = [(source, source ^ mask) for source in range(lax.axis_size(axis))]
    return lax.ppermute(value, axis, pairs)


def pair_mean(tensor):
    shape_in = tensor.shape
    paired = tensor.reshape(shape_in[:-2] + (shape_in[-2] // 2, 2, shape_in[-1]))
    return jnp.sum(paired, axis=-2) * 0.5


def spread_rows(grads, factor):
    shape_in = grads.shape
    wide = jnp.broadcast_to(grads[..., :, None, :], shape_in[:-1] + (factor, shape_in[-1])) * (
        1.0 / factor
    )
    return wide.reshape(shape_in[:-2] + (shape_in[-2] * factor, shape_in[-1]))


def body(queries, key_rows, value_rows, out_weight, cotangent, pattern):
    row_count, features = queries.shape
    blocks = row_count // BLK
    local_levels = blocks.bit_length() - 1
    seq_count = lax.axis_size("seq")
    cross_levels = seq_count.bit_length() - 1
    level_count = local_levels + cross_levels
    head_count = features // DH
    keys_all = (1 + level_count) * BLK
    score_scale = DH ** (-0.5)
    where_seq = lax.axis_index("seq")
    stacked = jnp.stack([key_rows, value_rows])
    coarse_base = (
        stacked.reshape(2, BLK, row_count // BLK, features).astype(jnp.float32).mean(axis=2)
    )
    siblings = []
    current = coarse_base
    for level_idx in range(cross_levels):
        received = swapped(current, "seq", level_idx)
        siblings.append(received)
        if level_idx + 1 < cross_levels:
            upper_half = jnp.right_shift(where_seq, level_idx) & 1 == 1
            joined = jnp.where(
                upper_half,
                jnp.concatenate([received, current], axis=1),
                jnp.concatenate([current, received], axis=1),
            )
            current = pair_mean(joined)
    segments = [stacked.reshape(2, blocks, BLK, features)]
    for level_idx in range(local_levels):
        factor = 2**level_idx
        group_count = blocks >> level_idx
        if level_idx == 0:
            pooled = stacked
        else:
            pooled = (
                stacked.reshape(2, row_count // factor, factor, features)
                .astype(jnp.float32)
                .mean(axis=2)
                .astype(jnp.bfloat16)
            )
        sibling = pooled.reshape(2, group_count // 2, 2, BLK, features)[:, :, ::-1].reshape(
            2, group_count, BLK, features
        )
        segments.append(
            jnp.broadcast_to(sibling[:, :, None], (2, group_count, factor, BLK, features)).reshape(
                2, blocks, BLK, features
            )
        )
    for level_idx in range(cross_levels):
        segments.append(
            jnp.broadcast_to(
                siblings[level_idx].astype(jnp.bfloat16)[:, None], (2, blocks, BLK, features)
            )
        )
    key_set = jnp.concatenate(segments, axis=2)
    key_bias = jnp.concatenate(
        [jnp.zeros((BLK,), jnp.float32)]
        + [jnp.full((BLK,), level_idx * LOG_TWO, jnp.float32) for level_idx in range(level_count)]
    )
    level_flags = pattern == 1
    kept_mask = jnp.concatenate(
        [
            jnp.ones((blocks, BLK), bool),
            jnp.broadcast_to(level_flags[:, :, None], (blocks, level_count, BLK)).reshape(
                blocks, level_count * BLK
            ),
        ],
        axis=1,
    )
    query_heads = queries.reshape(blocks, BLK, head_count, DH)
    key_heads = key_set[0].reshape(blocks, keys_all, head_count, DH)
    value_heads = key_set[1].reshape(blocks, keys_all, head_count, DH)
    scores = (
        jnp.einsum("bqhd,bkhd->bhqk", query_heads, key_heads, preferred_element_type=jnp.float32)
        * score_scale
        + key_bias
    )
    scores = jnp.where(kept_mask[:, None, None, :], scores, -jnp.inf)
    row_max = jnp.max(scores, axis=-1, keepdims=True)
    weights_raw = jnp.exp(scores - row_max)
    attn_prob = weights_raw / jnp.sum(weights_raw, axis=-1, keepdims=True)
    prob_low = attn_prob.astype(jnp.bfloat16)
    mixed = jnp.einsum("bhqk,bkhd->bqhd", prob_low, value_heads, preferred_element_type=jnp.float32)
    attended = mixed.astype(jnp.bfloat16).reshape(row_count, features)
    partial_out = jnp.dot(attended, out_weight, preferred_element_type=jnp.float32)
    output = lax.psum_scatter(partial_out, "head", scatter_dimension=1, tiled=True).astype(
        jnp.bfloat16
    )
    grads_full = lax.all_gather(cotangent, "head", axis=1, tiled=True)
    grad_attn = lax.dot_general(
        grads_full, out_weight, (((1,), (1,)), ((), ())), preferred_element_type=jnp.float32
    ).astype(jnp.bfloat16)
    grad_weight = lax.psum_scatter(
        lax.dot_general(
            grads_full, attended, (((0,), (0,)), ((), ())), preferred_element_type=jnp.float32
        ),
        "seq",
        scatter_dimension=0,
        tiled=True,
    )
    grad_heads = grad_attn.reshape(blocks, BLK, head_count, DH)
    grad_prob = jnp.einsum(
        "bqhd,bkhd->bhqk", grad_heads, value_heads, preferred_element_type=jnp.float32
    )
    row_delta = jnp.sum(attn_prob * grad_prob, axis=-1, keepdims=True)
    grad_score = (attn_prob * (grad_prob - row_delta)).astype(jnp.bfloat16)
    grad_query = (
        (
            jnp.einsum("bhqk,bkhd->bqhd", grad_score, key_heads, preferred_element_type=jnp.float32)
            * score_scale
        )
        .astype(jnp.bfloat16)
        .reshape(row_count, features)
    )
    grad_keyset = (
        jnp.einsum("bhqk,bqhd->bkhd", grad_score, query_heads, preferred_element_type=jnp.float32)
        * score_scale
    )
    grad_valset = jnp.einsum(
        "bhqk,bqhd->bkhd", prob_low, grad_heads, preferred_element_type=jnp.float32
    )
    grad_sets = jnp.stack([grad_keyset, grad_valset]).reshape(2, blocks, keys_all, features)
    token_grad = grad_sets[:, :, :BLK].reshape(2, row_count, features)
    for level_idx in range(local_levels):
        factor = 2**level_idx
        group_count = blocks >> level_idx
        lower = (level_idx + 1) * BLK
        segment = (
            grad_sets[:, :, lower : lower + BLK]
            .reshape(2, group_count, factor, BLK, features)
            .sum(axis=2)
        )
        restored = segment.reshape(2, group_count // 2, 2, BLK, features)[:, :, ::-1].reshape(
            2, group_count * BLK, features
        )
        token_grad = token_grad + spread_rows(restored, factor)
    sibling_grads = []
    for level_idx in range(cross_levels):
        lower = (local_levels + 1 + level_idx) * BLK
        sibling_grads.append(jnp.sum(grad_sets[:, :, lower : lower + BLK], axis=1))
    carried = jnp.zeros((2, BLK, features), jnp.float32)
    for level_idx in reversed(range(cross_levels)):
        outgoing = sibling_grads[level_idx]
        if level_idx + 1 < cross_levels:
            halves = spread_rows(carried, 2)
            lower_part = halves[:, :BLK]
            upper_part = halves[:, BLK:]
            upper_half = jnp.right_shift(where_seq, level_idx) & 1 == 1
            own_part = jnp.where(upper_half, upper_part, lower_part)
            outgoing = outgoing + jnp.where(upper_half, lower_part, upper_part)
        else:
            own_part = jnp.zeros_like(outgoing)
        carried = own_part + swapped(outgoing, "seq", level_idx)
    token_grad = token_grad + spread_rows(carried, 2**local_levels)
    grad_keys = token_grad[0].astype(jnp.bfloat16)
    grad_values = token_grad[1].astype(jnp.bfloat16)
    return (output, grad_query, grad_keys, grad_values, grad_weight)


def solution(mesh):
    placed = (
        P("seq", "head"),
        P("seq", "head"),
        P("seq", "head"),
        P("head", None),
        P("seq", "head"),
        P("seq", None),
    )
    return jax.shard_map(
        body,
        mesh=mesh,
        in_specs=placed,
        out_specs=(
            P("seq", "head"),
            P("seq", "head"),
            P("seq", "head"),
            P("seq", "head"),
            P("seq", "head"),
        ),
        check_vma=False,
    )
```

profile of v0, /device:TPU:0, one launch (start us, length us, event | category | flops | bytes accessed | tf_op | source)
XLA Modules:
  0.0 725.5 jit_solution(14627381544518607842)
XLA Ops:
  8.0 5.6 convert_reduce_fusion
  15.1 4.1 stack.48
  19.2 4.3 stack.51
  23.5 2.2 stack.49
  25.7 2.2 stack.52
  28.0 3.5 copy.195
  31.5 4.1 copy.170
  35.7 13.4 %convert_reduce_fusion.2 = f32[2,512,1024]{2,1,0:T(8,128)S(1)} fusion(bf16[1,512,2,1024]{3,2,1,0:T(2,128)(2,1)} %stack.49, bf16[1,512,2,1024]{3,2,1,0:T(2,128)(2,1)} %stack.48), kind=kLoop, calls=%fused_computation.44 | loop fusion | flops 5242880 | bytes 8388608 | tf_op jit(solution)/shard_map/reduce_sum | solution.py:73
  50.9 3.2 rev.17
  54.1 4.3 pad_maximum_fusion.1
  58.4 4.7 rev.16
  63.2 8.0 %convert_reduce_fusion.1 = f32[2,256,1024]{2,1,0:T(8,128)S(1)} fusion(bf16[1,256,4,1024]{3,2,1,0:T(4,128)(2,1)} %stack.52, bf16[1,256,4,1024]{3,2,1,0:T(4,128)(2,1)} %stack.51), kind=kLoop, calls=%fused_computation.43 | loop fusion | flops 5767168 | bytes 6291456 | tf_op jit(solution)/shard_map/reduce_sum | solution.py:73
  73.5 2.5 bitcast_reduce_fusion.2
  76.5 2.4 collective-permute-start.1
  79.0 2.7 maximum_dynamic-update-slice_fusion
  81.7 2.9 constant_dynamic-update-slice_fusion.2
  85.2 2.4 constant_dynamic-update-slice_fusion.1
  88.2 2.5 constant_dynamic-update-slice_fusion
  90.7 12.1 %collective-permute-done.1 = f32[2,128,1024]{2,0,1:T(2,128)S(1)} collective-permute-done((f32[2,128,1024]{2,0,1:T(2,128)S(1)}, f32[2,128,1024]{2,0,1:T(2,128)S(1)}, u32[]{:S(2)}, u32[]{:S(2)}) %collective-permute-start.1) | collective-permute-done | bytes 1048608 | tf_op jit(solution)/shard_map/ppermute | solution.py:18
  102.8 3.4 bitcast_reduce_fusion.1
  106.8 3.2 collective-permute-start.2
  110.0 2.6 broadcast_dynamic-update-slice_fusion.2
  113.1 2.6 broadcast_dynamic-update-slice_fusion.1
  115.7 17.6 %collective-permute-done.2 = bf16[2,128,1024]{2,0,1:T(2,128)(2,1)S(1)} collective-permute-done((bf16[2,128,1024]{2,0,1:T(2,128)(2,1)S(1)}, bf16[2,128,1024]{2,0,1:T(2,128)(2,1)S(1)}, u32[]{:S(2)}, u32[]{:S(2)}) %collective-permute-start.2) | collective-permute-done | bytes 524320 | tf_op jit(solution)/shard_map/ppermute | solution.py:18
  133.4 2.7 broadcast_dynamic-update-slice_fusion
  136.1 22.7 %fusion.37 = (bf16[1,8,896,1024]{3,2,1,0:T(8,128)(2,1)}, bf16[1,8,896,1024]{3,2,1,0:T(8,128)(2,1)}) fusion(bf16[2,8,896,1024]{3,2,1,0:T(8,128)(2,1)} %broadcast_dynamic-update-slice_fusion), kind=kLoop, calls=%fused_computation.91 | loop fusion | bytes 58720256 | tf_op jit(solution)/shard_map/slice | solution.py:106
  158.8 19.8 %copy.158 = bf16[1,8,896,1024]{2,3,1,0:T(8,128)(2,1)} copy(bf16[1,8,896,1024]{3,2,1,0:T(8,128)(2,1)} %get-tuple-element.42) | data formatting | bytes 29360128 | tf_op jit(solution)/shard_map/slice | solution.py:106
  178.6 20.2 %copy.156 = bf16[1,8,896,1024]{2,3,1,0:T(8,128)(2,1)} copy(bf16[1,8,896,1024]{3,2,1,0:T(8,128)(2,1)} %get-tuple-element.43) | data formatting | bytes 29360128 | tf_op jit(solution)/shard_map/slice | solution.py:107
  198.8 20.5 %fusion.39 = (f32[8,8,128]{2,1,0:T(8,128)S(1)}, f32[8,8,128,896]{2,3,1,0:T(8,128)}) fusion(f32[896]{0:T(1024)S(1)} %copy-done.9, pred[8,896]{1,0:T(8,128)(4,1)S(1)} %concatenate.29, bf16[8,896,8,128]{1,3,2,0:T(8,128)(2,1)} %bitcast.124, bf16[8,128,8,128]{1,3,2,0:T(8,128)(2,1)S(1)} %copy-done.3), kind=kOutput, calls=%fused_computation.93 | convolution fusion | flops 1915749248 | bytes 46180864 | tf_op jit(solution)/shard_map/sub | solution.py:115
  219.2 17.0 %convert_bitcast_fusion.1 = bf16[8,128,8,128]{1,3,2,0:T(8,128)(2,1)} fusion(bf16[8,896,8,128]{1,3,2,0:T(8,128)(2,1)} %bitcast.126, f32[8,8,128,896]{2,3,1,0:T(8,128)} %get-tuple-element.49, f32[8,8,128]{2,1,0:T(8,128)S(1)} %get-tuple-element.48), kind=kOutput, calls=%fused_computation.67 | convolution fusion | flops 1894776832 | bytes 46170112 | tf_op jit(solution)/shard_map/bhqk,bkhd->bqhd/dot_general | solution.py:118
  236.2 3.2 copy.162
  239.4 14.4 %fusion.27 = f32[1024,4096]{1,0:T(8,128)} fusion(bf16[1024,4096]{1,0:T(8,128)(2,1)} %param.9, bf16[128,8,8,128]{3,2,1,0:T(8,128)(2,1)S(1)} %bitcast.138), kind=kOutput, calls=%fused_computation.57 | convolution fusion | flops 8589934592 | bytes 27262976 | tf_op jit(solution)/shard_map/dot_general | solution.py:120
  253.9 14.8 %convolution_bitcast_fusion = f32[4096,1024]{0,1:T(8,128)} fusion(bf16[1024,4096]{1,0:T(8,128)(2,1)} %all-gather.2.cloned.1.call-done, bf16[128,8,8,128]{3,2,1,0:T(8,128)(2,1)S(1)} %bitcast.139), kind=kOutput, calls=%fused_computation.26 | convolution fusion | flops 8589934592 | bytes 27262976 | tf_op jit(solution)/shard_map/dot_general | solution.py:129
  268.8 14.0 %convert_bitcast_fusion = bf16[128,8,8,128]{3,1,2,0:T(8,128)(2,1)S(1)} fusion(bf16[1024,4096]{1,0:T(8,128)(2,1)} %all-gather.2.cloned.1.call-done, bf16[1024,4096]{1,0:T(8,128)(2,1)} %param.9), kind=kOutput, calls=%fused_computation.66 | convolution fusion | flops 8590983168 | bytes 18874368 | tf_op jit(solution)/shard_map/dot_general | solution.py:125
  283.4 2.8 copy.173
  286.3 26.5 %multiply_reduce_fusion = (f32[8,8,128]{2,1,0:T(8,128)S(1)}, f32[8,8,128,896]{2,3,1,0:T(8,128)}) fusion(f32[8,8,128,896]{2,3,1,0:T(8,128)} %get-tuple-element.49, f32[8,8,128]{2,1,0:T(8,128)S(1)} %get-tuple-element.48, bf16[8,128,8,128]{1,3,2,0:T(8,128)(2,1)} %copy.173, bf16[8,896,8,128]{1,3,2,0:T(8,128)(2,1)} %bitcast.127), kind=kOutput, calls=%fused_computation.19 | convolution fusion | flops 1901060096 | bytes 75563008 | tf_op jit(solution)/shard_map/bqhd,bkhd->bhqk/dot_general | solution.py:137
  312.7 26.9 %multiply_convert_fusion = bf16[8,8,128,896]{2,3,1,0:T(8,128)(2,1)} fusion(f32[8,8,128,896]{2,3,1,0:T(8,128)} %get-tuple-element.51, f32[8,8,128]{2,1,0:T(8,128)S(1)} %get-tuple-element.50, f32[8,8,128,896]{2,3,1,0:T(8,128)} %get-tuple-element.49, f32[8,8,128]{2,1,0:T(8,128)S(1)} %get-tuple-element.48), kind=kLoop, calls=%fused_computation.18 | loop fusion | flops 29360128 | bytes 73465856 | tf_op jit(solution)/shard_map/convert_element_type | solution.py:141
  339.7 15.2 %multiply_bitcast_fusion = f32[8,896,8,128]{3,1,2,0:T(8,128)} fusion(bf16[8,8,128,896]{2,3,1,0:T(8,128)(2,1)} %multiply_convert_fusion, bf16[8,128,8,128]{1,3,2,0:T(8,128)(2,1)S(1)} %copy-done.4), kind=kOutput, calls=%fused_computation.17 | convolution fusion | flops 1886388224 | bytes 46137344 | tf_op jit(solution)/shard_map/bhqk,bqhd->bkhd/dot_general | solution.py:151
  354.9 31.3 %copy.172 = f32[8,896,8,128]{1,3,2,0:T(8,128)} copy(f32[8,896,8,128]{3,1,2,0:T(8,128)} %multiply_bitcast_fusion) | data formatting | bytes 58720256 | tf_op jit(solution)/shard_map/mul | solution.py:151
  386.2 19.9 %fusion.21 = f32[8,8,128,896]{3,2,1,0:T(8,128)} fusion(bf16[8,128,8,128]{1,3,2,0:T(8,128)(2,1)S(1)} %copy-done.7, f32[8,8,128,896]{2,3,1,0:T(8,128)} %get-tuple-element.49, f32[8,8,128]{2,1,0:T(8,128)S(1)} %get-tuple-element.48), kind=kOutput, calls=%fused_computation.45 | convolution fusion | flops 1893728256 | bytes 60850176 | tf_op jit(solution)/shard_map/bhqk,bqhd->bkhd/dot_general | solution.py:154
  406.0 33.1 %fusion.16 = (f32[2,128,1024]{1,2,0:T(8,128)S(1)}, f32[2,128,1024]{1,2,0:T(8,128)S(1)}, f32[2,128,1024]{1,2,0:T(8,128)S(1)}, f32[2,8,128,1024]{2,3,1,0:T(8,128)}...) fusion(f32[1,8,896,1024]{2,3,1,0:T(8,128)} %bitcast.106, ...), kind=kLoop, calls=%fused_computation.34 | loop fusion | flops 20185088 | bytes 95420416 | tf_op jit(solution)/shard_map/reduce_sum | solution.py:175
  442.1 89.0 %collective-permute-done.3 = f32[2,128,1024]{2,0,1:T(2,128)S(1)} collective-permute-done((f32[2,128,1024]{2,0,1:T(2,128)}, f32[2,128,1024]{2,0,1:T(2,128)S(1)}, u32[]{:S(2)}, u32[]{:S(2)}) %collective-permute-start.3) | collective-permute-done | bytes 1048608 | tf_op jit(solution)/shard_map/ppermute | solution.py:18
  532.4 3.0 select_add_fusion.1
  536.7 48.1 %collective-permute-done.4 = f32[2,128,1024]{2,0,1:T(2,128)} collective-permute-done((f32[2,128,1024]{2,0,1:T(2,128)}, f32[2,128,1024]{2,0,1:T(2,128)}, u32[]{:S(2)}, u32[]{:S(2)}) %collective-permute-start.4) | collective-permute-done | bytes 1048608 | tf_op jit(solution)/shard_map/ppermute | solution.py:18
  590.0 14.9 %fusion.25 = bf16[8,128,8,128]{1,3,2,0:T(8,128)(2,1)} fusion(bf16[8,896,8,128]{1,3,2,0:T(8,128)(2,1)} %bitcast.125, bf16[8,8,128,896]{2,3,1,0:T(8,128)(2,1)} %multiply_convert_fusion), kind=kOutput, calls=%fused_computation.54 | convolution fusion | flops 1881145344 | bytes 31457280 | tf_op jit(solution)/shard_map/bhqk,bkhd->bqhd/dot_general | solution.py:144
  604.9 4.3 copy.168
  609.2 3.5 copy.213
  612.7 5.5 reduce_sum.120
  618.2 6.6 reduce_sum.119
  624.8 5.4 copy.177
  630.2 3.1 reverse_multiply_fusion.1
  633.3 2.9 copy.178
  636.2 2.6 reverse_multiply_fusion
  638.9 4.6 broadcast_in_dim.48
  643.5 10.9 %reshape.162 = f32[2,1024,1024]{2,1,0:T(8,128)} reshape(f32[2,512,2,1024]{3,2,1,0:T(2,128)} %broadcast_in_dim.48) | data formatting | bytes 16777216 | tf_op jit(solution)/shard_map/reshape | solution.py:32
  654.3 7.2 broadcast_in_dim.49
  661.5 10.0 %reshape.164 = f32[2,1024,1024]{2,1,0:T(8,128)} reshape(f32[2,256,4,1024]{3,2,1,0:T(4,128)} %broadcast_in_dim.49) | data formatting | bytes 16777216 | tf_op jit(solution)/shard_map/reshape | solution.py:32
  671.6 8.7 %copy.175 = f32[2,8,128,1024]{3,2,1,0:T(8,128)} copy(f32[2,8,128,1024]{2,3,1,0:T(8,128)} %get-tuple-element.40) | data formatting | bytes 16777216 | tf_op jit(solution)/shard_map/slice | solution.py:158
  680.2 7.4 %rev.19 = f32[2,4,2,128,1024]{3,4,2,1,0:T(8,128)} reverse(f32[2,4,2,128,1024]{3,4,2,1,0:T(8,128)} %bitcast.113), dimensions={2} | reverse | bytes 16777216 | tf_op jit(solution)/shard_map/rev | solution.py:168
  687.6 8.7 %copy.176 = f32[2,4,2,128,1024]{4,3,2,1,0:T(8,128)} copy(f32[2,4,2,128,1024]{3,4,2,1,0:T(8,128)} %rev.19) | data formatting | bytes 16777216 | tf_op jit(solution)/shard_map/rev | solution.py:168
  697.1 12.5 %fusion.18 = bf16[2,1024,1024]{2,1,0:T(8,128)(2,1)S(1)} fusion(f32[2,1024,1024]{2,1,0:T(8,128)} %reshape.164, f32[2,1024,1024]{2,1,0:T(8,128)} %reshape.162, f32[2,4,2,128,1024]{4,3,2,1,0:T(8,128)} %copy.176, f32[2,8,128,1024]{3,2,1,0:T(8,128)} %copy.175, f32[2,128,1024]{2,1,0:T(8,128)S(1)} %add_multiply_fusion), kind=kLoop, calls=%fused_computation.38 | loop fusion | flops 10485760 | bytes 38797312 | tf_op jit(solution)/shard_map/convert.1
  709.6 2.4 slice_bitcast_fusion
  712.1 3.8 convert_element_type.83
  715.9 2.9 copy.184
  (63 shorter events, 21.6 us)
Async XLA Ops:
  7.2 246.8 %all-gather.2.cloned.1.call-start = ((), (), s32[]{:S(2)}) async-start(), calls=%async_computation.3 | async-start | bytes 10485760 | tf_op jit(solution)/shard_map/all_gather | solution.py:124
  7.9 15.6 %copy-start = (bf16[1024,1024]{1,0:T(8,128)(2,1)S(1)}, bf16[1024,1024]{1,0:T(8,128)(2,1)}, u32[]{:S(2)}) copy-start(bf16[1024,1024]{1,0:T(8,128)(2,1)} %param.8) | copy-start | bytes 6291460
  7.9 704.2 %reduce-scatter.3.cloned.1.call-start = ((), (), s32[]{:S(2)}) async-start(), calls=%async_computation.2 | async-start | bytes 20971520 | tf_op jit(solution)/shard_map/reduce_scatter | solution.py:121
  14.7 56.8 %collective-permute-start = (f32[2,128,1024]{2,1,0:T(8,128)}, f32[2,128,1024]{2,1,0:T(8,128)S(1)}, u32[]{:S(2)}, u32[]{:S(2)}) collective-permute-start(f32[2,128,1024]{2,1,0:T(8,128)} %broadcast_multiply_fusion.3), channel_id=1, source_target_pairs={{0,4},{4,0},{8,12},{12,8},{16,20},{20,16},{24,28},{28,24},{1,5},{5... | collective-permute-start | bytes 3145736 | tf_op jit(solution)/shard_map/ppermute | solution.py:18
  15.1 12.8 %copy-start.8 = (s32[8,6]{1,0:T(8,128)S(1)}, s32[8,6]{1,0:T(8,128)}, u32[]{:S(2)}) copy-start(s32[8,6]{1,0:T(8,128)} %param.11) | copy-start | bytes 580
  71.2 7.8 %copy-start.1 = (bf16[1024,1024]{1,0:T(8,128)(2,1)S(1)}, bf16[1024,1024]{1,0:T(8,128)(2,1)}, u32[]{:S(2)}) copy-start(bf16[1024,1024]{1,0:T(8,128)(2,1)} %param.7) | copy-start | bytes 6291460
  73.5 8.2 %copy-start.2 = (bf16[2,4,2,128,1024]{4,3,2,1,0:T(8,128)(2,1)S(1)}, bf16[2,4,2,128,1024]{4,3,2,1,0:T(8,128)(2,1)}, u32[]{:S(2)}) copy-start(bf16[2,4,2,128,1024]{4,3,2,1,0:T(8,128)(2,1)} %rev.16) | copy-start | bytes 12582916
  76.5 26.3 %collective-permute-start.1 = (f32[2,128,1024]{2,0,1:T(2,128)S(1)}, f32[2,128,1024]{2,0,1:T(2,128)S(1)}, u32[]{:S(2)}, u32[]{:S(2)}) collective-permute-start(f32[2,128,1024]{2,0,1:T(2,128)S(1)} %broadcast_multiply_fusion.2), channel_id=1, source_target_pairs={{0,8},{4,12},{8,0},{12,4},{16,24},{20,28},{24,16},{28,20},{1,9},{5... | collective-permute-start | bytes 3145736 | tf_op jit(solution)/shard_map/ppermute | solution.py:18
  79.0 5.6 copy-start.5
  106.8 26.5 %collective-permute-start.2 = (bf16[2,128,1024]{2,0,1:T(2,128)(2,1)S(1)}, bf16[2,128,1024]{2,0,1:T(2,128)(2,1)S(1)}, u32[]{:S(2)}, u32[]{:S(2)}) collective-permute-start(bf16[2,128,1024]{2,0,1:T(2,128)(2,1)S(1)} %broadcast_multiply_fusion.1), channel_id=1, source_target_pairs={{0,16},{4,20},{8,24},{12,28},{16,0},{20,4},{24,8},{28,12},{1,17},{... | collective-permute-start | bytes 1572872 | tf_op jit(solution)/shard_map/ppermute | solution.py:18
  178.6 20.2 %copy-start.3 = (bf16[8,128,8,128]{1,3,2,0:T(8,128)(2,1)S(1)}, bf16[8,128,8,128]{1,3,2,0:T(8,128)(2,1)}, u32[]{:S(2)}) copy-start(bf16[8,128,8,128]{1,3,2,0:T(8,128)(2,1)} %copy.170) | copy-start | bytes 6291460
  178.6 20.2 %copy-start.9 = (f32[896]{0:T(1024)S(1)}, f32[896]{0:T(1024)}, u32[]{:S(2)}) copy-start(f32[896]{0:T(1024)} %constant.8.clone.1) | copy-start | bytes 10756
  253.9 462.0 %reduce-scatter.5.cloned.1.call-start = ((), (), s32[]{:S(2)}) async-start(), calls=%async_computation.4 | async-start | bytes 18874368 | tf_op jit(solution)/shard_map/reduce_scatter | solution.py:128
  312.7 27.0 %copy-start.4 = (bf16[8,128,8,128]{1,3,2,0:T(8,128)(2,1)S(1)}, bf16[8,128,8,128]{1,3,2,0:T(8,128)(2,1)}, u32[]{:S(2)}) copy-start(bf16[8,128,8,128]{1,3,2,0:T(8,128)(2,1)} %copy.170) | copy-start | bytes 6291460
  354.9 31.3 %copy-start.7 = (bf16[8,128,8,128]{1,3,2,0:T(8,128)(2,1)S(1)}, bf16[8,128,8,128]{1,3,2,0:T(8,128)(2,1)}, u32[]{:S(2)}) copy-start(bf16[8,128,8,128]{1,3,2,0:T(8,128)(2,1)} %copy.173) | copy-start | bytes 6291460
  440.5 90.7 %collective-permute-start.3 = (f32[2,128,1024]{2,0,1:T(2,128)}, f32[2,128,1024]{2,0,1:T(2,128)S(1)}, u32[]{:S(2)}, u32[]{:S(2)}) collective-permute-start(f32[2,128,1024]{2,0,1:T(2,128)} %copy.179), channel_id=1, source_target_pairs={{0,16},{4,20},{8,24},{12,28},{16,0},{20,4},{24,8},{28,12},{1,17},{... | collective-permute-start | bytes 3145736 | tf_op jit(solution)/shard_map/ppermute | solution.py:18
  535.4 49.4 %collective-permute-start.4 = (f32[2,128,1024]{2,0,1:T(2,128)}, f32[2,128,1024]{2,0,1:T(2,128)}, u32[]{:S(2)}, u32[]{:S(2)}) collective-permute-start(f32[2,128,1024]{2,0,1:T(2,128)} %select_add_fusion.1), channel_id=1, source_target_pairs={{0,8},{4,12},{8,0},{12,4},{16,24},{20,28},{24,16},{28,20},{1,9},{5... | collective-permute-start | bytes 3145736 | tf_op jit(solution)/shard_map/ppermute | solution.py:18
  536.7 51.6 %copy-start.6 = (f32[2,128,1024]{2,1,0:T(8,128)S(1)}, f32[2,128,1024]{2,1,0:T(8,128)}, u32[]{:S(2)}) copy-start(f32[2,128,1024]{2,1,0:T(8,128)} %copy.183) | copy-start | bytes 3145732
  590.0 106.4 %collective-permute-start.5 = (f32[2,128,1024]{2,1,0:T(8,128)}, f32[2,128,1024]{2,1,0:T(8,128)S(1)}, u32[]{:S(2)}, u32[]{:S(2)}) collective-permute-start(f32[2,128,1024]{2,1,0:T(8,128)} %select_add_fusion), channel_id=1, source_target_pairs={{0,4},{4,0},{8,12},{12,8},{16,20},{20,16},{24,28},{28,24},{1,5},{5... | collective-permute-start | bytes 3145736 | tf_op jit(solution)/shard_map/ppermute | solution.py:18
Sparse Core Ops, SparseCore 0:
  9.8 90.2 all-gather.1
  254.0 155.0 reduce-scatter.2
  411.4 224.0 reduce-scatter.4
where the time goes:
time: 735 us; the launch traced here: 725 us
  local copies, waits for them, and re-layouts  232 us (32%)
  waiting for transfers between devices  167 us (23%)
  matrix products  157 us (21%)
  other arithmetic  149 us (20%)
  between operations  14.2 us (2%)
    ppermute x6, waiting for transfers between devices, swapped(): return lax.ppermute(value, axis, pairs)  167 us
    slice x2, local copies, waits for them, and re-layouts, body(): key_heads = key_set[0].reshape(blocks, keys_all, head_count, DH)  42.5 us
    reduce_sum x1, other arithmetic, body(): sibling_grads.append(jnp.sum(grad_sets[:, :, lower:lower + BLK], axis=1))  33.1 us
    mul x1, local copies, waits for them, and re-layouts, body(): jnp.einsum('bhqk,bqhd->bkhd', grad_score, query_heads, preferred_element_...  31.3 us
    convert_element_type x1, other arithmetic, body(): grad_score = (attn_prob * (grad_prob - row_delta)).astype(jnp.bfloat16)  26.9 us
    dot_general x1, matrix products, body(): jnp.einsum('bqhd,bkhd->bhqk', grad_heads, value_heads, preferred_element_...  26.5 us
    unnamed x29, local copies, waits for them, and re-layouts  23.7 us
    reduce_sum x2, other arithmetic, body(): pooled = stacked.reshape(2, row_count // factor, factor, features).astype...  21.4 us
  transfers between devices with their start and end apart: 9, of which 4 were waited for; matrix products, arithmetic and copies ran while one was open for 74% of the time, Pallas kernels for 0%

commit v1 on v0

v1 whole, which is shorter than its diff:
```python
import functools
import math

import jax
import jax.numpy as jnp
from jax import lax
from jax.experimental import pallas as pl
from jax.experimental.pallas import tpu as pltpu
from jax.sharding import PartitionSpec as P

DH = 128
BLK = 128
PAIR = 2 * BLK
QUAD = 4 * BLK
SCALE = DH ** (-0.5)
LOG2E = 1.0 / math.log(2.0)
DROPPED = -1e30
VMEM = 44 * 1024 * 1024

NT = (((1,), (1,)), ((), ()))
TN = (((0,), (0,)), ((), ()))


def dot(left, right, dims=(((1,), (0,)), ((), ()))):
    return lax.dot_general(left, right, dims, preferred_element_type=jnp.float32)


def swapped(value, axis, mask):
    pairs = [(source, source ^ mask) for source in range(lax.axis_size(axis))]
    return lax.ppermute(value, axis, pairs)


def mean_matrix(rows, factor):
    group = lax.broadcasted_iota(jnp.int32, (rows, rows * factor), 0)
    token = lax.broadcasted_iota(jnp.int32, (rows, rows * factor), 1)
    return jnp.where(token // factor == group, 1.0 / factor, 0.0).astype(jnp.bfloat16)


def key_sets(rows, pool_two, pool_four, far):
    pairs = rows.shape[0] // PAIR
    quads = rows.shape[0] // QUAD
    twos = [
        dot(pool_two, rows[i * PAIR : (i + 1) * PAIR]).astype(jnp.bfloat16) for i in range(pairs)
    ]
    fours = [
        dot(pool_four, rows[i * QUAD : (i + 1) * QUAD]).astype(jnp.bfloat16) for i in range(quads)
    ]
    return [
        jnp.concatenate(
            [rows[i * PAIR : (i + 1) * PAIR], twos[i ^ 1], fours[(i >> 1) ^ 1], far], axis=0
        )
        for i in range(pairs)
    ]


def forward_kernel(q_ref, k_ref, v_ref, far_ref, two_ref, four_ref, bias_ref, prob_ref, out_ref):
    pool_two, pool_four = two_ref[...], four_ref[...]
    keys = key_sets(k_ref[...], pool_two, pool_four, far_ref[0])
    values = key_sets(v_ref[...], pool_two, pool_four, far_ref[1])
    for pair in range(len(keys)):
        span = slice(pair * PAIR, (pair + 1) * PAIR)
        scores = dot(keys[pair], q_ref[span, :], NT)
        parts = []
        for seg in range(scores.shape[0] // BLK):
            parts.append(
                scores[seg * BLK : (seg + 1) * BLK] * (SCALE * LOG2E)
                + bias_ref[pair, seg : seg + 1, :]
            )
        top = functools.reduce(jnp.maximum, [jnp.max(x, axis=0, keepdims=True) for x in parts])
        parts = [jnp.exp2(x - top) for x in parts]
        total = functools.reduce(jnp.add, [jnp.sum(x, axis=0, keepdims=True) for x in parts])
        scale = 1.0 / total
        prob = jnp.concatenate([(x * scale).astype(jnp.bfloat16) for x in parts], axis=0)
        prob_ref[0, pair] = prob
        out_ref[span, :] = dot(values[pair], prob, TN).T.astype(jnp.bfloat16)


def backward_kernel(
    q_ref, k_ref, v_ref, g_ref, far_ref, two_ref, four_ref, prob_ref, dq_ref, dk_ref, dv_ref, dfar_ref
):
    pool_two, pool_four = two_ref[...], four_ref[...]
    keys = key_sets(k_ref[...], pool_two, pool_four, far_ref[0])
    values = key_sets(v_ref[...], pool_two, pool_four, far_ref[1])
    grad_keys, grad_values = [], []
    for pair in range(len(keys)):
        span = slice(pair * PAIR, (pair + 1) * PAIR)
        grads = g_ref[span, :]
        grad_prob = dot(values[pair], grads, NT)
        prob_low = prob_ref[0, pair]
        prob = prob_low.astype(jnp.float32)
        delta = jnp.sum(prob * grad_prob, axis=0, keepdims=True)
        grad_score = (prob * (grad_prob - delta)).astype(jnp.bfloat16)
        dq_ref[span, :] = (dot(keys[pair], grad_score, TN) * SCALE).T.astype(jnp.bfloat16)
        grad_keys.append(dot(grad_score, q_ref[span, :]) * SCALE)
        grad_values.append(dot(prob_low, grads))
    for slot, (grad_sets, token_ref) in enumerate(((grad_keys, dk_ref), (grad_values, dv_ref))):
        dfar_ref[slot] = functools.reduce(
            jnp.add, [grad[PAIR + 2 * BLK :] for grad in grad_sets]
        ).astype(jnp.bfloat16)
        spread_four = []
        for quad in range(len(grad_sets) // 2):
            first = 2 * (quad ^ 1)
            node = sum(grad_sets[i][PAIR + BLK : PAIR + 2 * BLK] for i in (first, first + 1))
            spread_four.append(dot(pool_four, node.astype(jnp.bfloat16), TN))
        for pair in range(len(grad_sets)):
            node = grad_sets[pair ^ 1][PAIR : PAIR + BLK].astype(jnp.bfloat16)
            half = (pair & 1) * PAIR
            token_ref[pair * PAIR : (pair + 1) * PAIR, :] = (
                grad_sets[pair][:PAIR]
                + dot(pool_two, node, TN)
                + spread_four[pair >> 1][half : half + PAIR]
            )


def body(queries, key_rows, value_rows, out_weight, cotangent, pattern):
    rows, features = queries.shape
    width = out_weight.shape[1]
    blocks = rows // BLK
    pairs = blocks // 2
    seq_count = lax.axis_size("seq")
    head_axis = lax.axis_size("head")
    cross_levels = seq_count.bit_length() - 1
    heads = features // DH
    far_rows = cross_levels * BLK
    keys_all = PAIR + 2 * BLK + far_rows
    segments = keys_all // BLK
    where_seq = lax.axis_index("seq")
    where_head = lax.axis_index("head")
    messages = [
        (2**level + i, level, BLK >> level) for level in range(cross_levels) for i in range(2**level)
    ]

    grads_full = lax.all_gather(cotangent, "head", axis=1, tiled=True)

    pools = [mean_matrix(BLK >> level, blocks << level) for level in range(cross_levels)]
    far_own = []
    for pool in pools:
        far_own.append(
            jnp.stack([dot(pool, key_rows), dot(pool, value_rows)]).astype(jnp.bfloat16)
        )
    far = jnp.concatenate(
        [swapped(far_own[level], "seq", mask) for mask, level, _ in messages], axis=1
    )

    pool_two, pool_four = mean_matrix(BLK, 2), mean_matrix(BLK, 4)
    kept = jnp.where(
        pattern == 1, jnp.arange(pattern.shape[1], dtype=jnp.float32), DROPPED
    ).reshape(pairs, 2, pattern.shape[1])
    own = jnp.zeros((pairs, 1), jnp.float32)
    first = jnp.stack([own, kept[:, 1, :1]], axis=-1)
    second = jnp.stack([kept[:, 0, :1], own], axis=-1)
    bias = jnp.concatenate([first, second, kept[:, :, 1:].transpose(0, 2, 1)], axis=1)
    bias = jnp.repeat(bias, BLK, axis=2)

    column = pl.BlockSpec((rows, DH), lambda h: (0, h))
    far_spec = pl.BlockSpec((2, far_rows, DH), lambda h: (0, 0, h))
    two_spec = pl.BlockSpec((BLK, PAIR), lambda h: (0, 0))
    four_spec = pl.BlockSpec((BLK, QUAD), lambda h: (0, 0))
    prob_spec = pl.BlockSpec((1, pairs, keys_all, PAIR), lambda h: (h, 0, 0, 0))
    work = 2 * heads * pairs * keys_all * PAIR * DH

    prob, attended = pl.pallas_call(
        forward_kernel,
        grid=(heads,),
        out_shape=(
            jax.ShapeDtypeStruct((heads, pairs, keys_all, PAIR), jnp.bfloat16),
            jax.ShapeDtypeStruct((rows, features), jnp.bfloat16),
        ),
        in_specs=[
            column,
            column,
            column,
            far_spec,
            two_spec,
            four_spec,
            pl.BlockSpec((pairs, segments, PAIR), lambda h: (0, 0, 0)),
        ],
        out_specs=(prob_spec, column),
        compiler_params=pltpu.CompilerParams(vmem_limit_bytes=VMEM),
        cost_estimate=pl.CostEstimate(
            flops=12 * work, bytes_accessed=24 * rows * features, transcendentals=0
        ),
        name="forward_attention",
    )(queries, key_rows, value_rows, far, pool_two, pool_four, bias)

    output = None
    share = width // head_axis
    for mask in reversed(range(head_axis)):
        target = where_head ^ mask
        weight = lax.dynamic_slice_in_dim(out_weight, target * share, share, 1)
        partial = dot(attended, weight)
        if mask:
            partial = swapped(partial.astype(jnp.bfloat16), "head", mask).astype(jnp.float32)
        output = partial if output is None else output + partial
    output = output.astype(jnp.bfloat16)

    core = where_seq & 1
    chip = where_seq >> 1
    chips = seq_count // 2
    piece = width // seq_count
    by_core = grads_full.reshape(rows, chips, 2, piece)

    def weight_grad(which):
        chosen = lax.dynamic_index_in_dim(by_core, which, 2, keepdims=False)
        return dot(chosen.reshape(rows, chips * piece), attended, TN)

    theirs = swapped(weight_grad(1 - core).astype(jnp.bfloat16), "seq", 1)
    mine = weight_grad(core)
    grad_attn = dot(grads_full, out_weight, NT).astype(jnp.bfloat16)
    theirs, grad_attn = lax.optimization_barrier((theirs, grad_attn))
    mine = (mine + theirs.astype(jnp.float32)).astype(jnp.bfloat16)
    mine = mine.reshape(chips, piece, features)
    parts = [
        lax.dynamic_index_in_dim(mine, chip ^ mask, 0, keepdims=False) for mask in range(chips)
    ]
    parts, grad_attn = lax.optimization_barrier((parts, grad_attn))
    arrived = [swapped(parts[mask], "seq", 2 * mask) for mask in range(1, chips)]

    grad_query, dk, dv, dfar = pl.pallas_call(
        backward_kernel,
        grid=(heads,),
        out_shape=(
            jax.ShapeDtypeStruct((rows, features), jnp.bfloat16),
            jax.ShapeDtypeStruct((rows, features), jnp.float32),
            jax.ShapeDtypeStruct((rows, features), jnp.float32),
            jax.ShapeDtypeStruct((2, far_rows, features), jnp.bfloat16),
        ),
        in_specs=[column, column, column, column, far_spec, two_spec, four_spec, prob_spec],
        out_specs=(column, column, column, far_spec),
        compiler_params=pltpu.CompilerParams(vmem_limit_bytes=VMEM),
        cost_estimate=pl.CostEstimate(
            flops=16 * work, bytes_accessed=36 * rows * features, transcendentals=0
        ),
        name="backward_attention",
    )(queries, key_rows, value_rows, grad_attn, far, pool_two, pool_four, prob)

    arrived, dfar = lax.optimization_barrier((arrived, dfar))
    grad_weight = parts[0].astype(jnp.float32)
    for part in arrived:
        grad_weight = grad_weight + part.astype(jnp.float32)
    returned, at = [], 0
    for mask, level, count in messages:
        returned.append(swapped(dfar[:, at : at + count], "seq", mask))
        at += count
    returned = jnp.concatenate(returned, axis=1)
    spread = jnp.concatenate([pools[level] for _, level, _ in messages], axis=0)
    grad_keys = (dk + dot(spread, returned[0], TN)).astype(jnp.bfloat16)
    grad_values = (dv + dot(spread, returned[1], TN)).astype(jnp.bfloat16)
    return (output, grad_query, grad_keys, grad_values, grad_weight)


def solution(mesh):
    placed = (
        P("seq", "head"),
        P("seq", "head"),
        P("seq", "head"),
        P("head", None),
        P("seq", "head"),
        P("seq", None),
    )
    return jax.shard_map(
        body,
        mesh=mesh,
        in_specs=placed,
        out_specs=(
            P("seq", "head"),
            P("seq", "head"),
            P("seq", "head"),
            P("seq", "head"),
            P("seq", "head"),
        ),
        check_vma=False,
    )
```

time: 735 us -> 361 us (0.49); the launches traced: 725 us -> 360 us
  local copies, waits for them, and re-layouts: 232 us -> 19.3 us
  other arithmetic: 149 us -> 7.46 us
  matrix products: 157 us -> 56.7 us
  Pallas kernels: 0 us -> 66.1 us
  starting transfers between devices: 6.21 us -> 50 us
  waiting for transfers between devices: 167 us -> 146 us
    dot_general x8 -> x15, matrix products: 137 us -> 56.7 us  [dot(): lax.dot_general(left, right, dims, preferred_element_type=jnp.float32)]
    reduce_sum x8 -> x0, other arithmetic: 78.2 us -> none  [the longest x1 33.1 us: body(): sibling_grads.append(jnp.sum(grad_sets[:, :, lower:lower + BLK], axis=1))]
    slice x5 -> x3, local copies, waits for them, and re-layouts: 72.1 us -> 0.11 us  [body(): returned.append(swapped(dfar[:, at:at + count], 'seq', mask))]
    ppermute x6 -> x21, waiting for transfers between devices: 167 us -> 97.7 us  [swapped(): return lax.ppermute(value, axis, pairs)]
    pallas_call x0 -> x2, Pallas kernels: none -> 66.1 us  [the longest x1 36 us: body(): pl.pallas_call(backward_kernel, grid=(heads,), out_shape=(jax.ShapeDtypeS...]
    all_gather x1, waiting for transfers between devices: 0.02 us -> 48.4 us  [body(): grads_full = lax.all_gather(cotangent, 'head', axis=1, tiled=True)]
    ppermute x6 -> x21, starting transfers between devices: 6.1 us -> 50 us  [swapped(): return lax.ppermute(value, axis, pairs)]
    mul x2 -> x0, local copies, waits for them, and re-layouts: 34.2 us -> none  [the longest x1 31.3 us: body(): jnp.einsum('bhqk,bqhd->bkhd', grad_score, query_heads, preferred_element_...]
  transfers between devices with their start and end apart: 9 -> 22, of which waited for: 4 -> 9; matrix products, arithmetic and copies ran while one was open for 74% -> 17% of each run, Pallas kernels for 0% -> 18%
where the time goes in v1:
time: 361 us; the launch traced here: 360 us
  waiting for transfers between devices  146 us (40%)
  Pallas kernels  66.1 us (18%)
  matrix products  56.7 us (16%)
  starting transfers between devices  50 us (14%)
  local copies, waits for them, and re-layouts  19.3 us (5%)
  between operations  14.7 us (4%)
  other arithmetic  7.46 us (2%)
    ppermute x21, waiting for transfers between devices, swapped(): return lax.ppermute(value, axis, pairs)  97.7 us
    dot_general x15, matrix products, dot(): lax.dot_general(left, right, dims, preferred_element_type=jnp.float32)  56.7 us
    ppermute x21, starting transfers between devices, swapped(): return lax.ppermute(value, axis, pairs)  50 us
    all_gather x1, waiting for transfers between devices, body(): grads_full = lax.all_gather(cotangent, 'head', axis=1, tiled=True)  48.4 us
    pallas_call x1, Pallas kernels, body(): pl.pallas_call(backward_kernel, grid=(heads,), out_shape=(jax.ShapeDtypeS...  36 us
    pallas_call x1, Pallas kernels, body(): pl.pallas_call(forward_kernel, grid=(heads,), out_shape=(jax.ShapeDtypeSt...  30.1 us
    unnamed x64, local copies, waits for them, and re-layouts  10.4 us
  transfers between devices with their start and end apart: 22, of which 9 were waited for; matrix products, arithmetic and copies ran while one was open for 17% of the time, Pallas kernels for 18%

profile of v1, /device:TPU:0, one launch (start us, length us, event | category | flops | bytes accessed | tf_op | source)
XLA Modules:
  0.0 360.4 jit_solution(14161719857909698307)
XLA Ops:
  7.2 3.9 %copy.22 = bf16[1024,1024]{0,1:T(8,128)(2,1)} copy(bf16[1024,1024]{1,0:T(8,128)(2,1)} %param.10) | data formatting | bytes 4194304 | tf_op args[4]
  11.2 2.2 fusion.24
  13.4 0.5 fusion.23
  13.9 4.6 %collective-permute-start.6 = (bf16[2,32,1024]{2,1,0:T(8,128)(2,1)S(1)}, bf16[2,32,1024]{2,1,0:T(8,128)(2,1)}, u32[]{:S(2)}, u32[]{:S(2)}) collective-permute-start(bf16[2,32,1024]{2,1,0:T(8,128)(2,1)S(1)} %pad_maximum_fusion.2), channel_id=1, source_target_pairs={{0,28},{4,24},{8,20},{12,16},{16,12},{20,8},{24,4},{28,0},{1,29},{... | collective-permute-start | bytes 393224 | tf_op jit(solution)/shard_map/ppermute | solution.py:30
  18.5 0.6 collective-permute-start.5
  19.1 0.5 fusion.22
  19.6 0.5 fusion.21
  20.1 0.7 pad_maximum_fusion.1
  20.9 1.7 collective-permute-start.1
  22.6 0.5 fusion.20
  23.0 0.4 fusion.19
  23.6 0.3 collective-permute-start
  24.0 0.1 slice_bitcast_fusion.4
  24.0 0.1 fusion.67
  24.1 0.1 copy.20
  24.2 0.1 broadcast_in_dim.63
  24.4 1.1 collective-permute-done
  25.6 1.9 collective-permute-start.4
  27.5 13.2 %collective-permute-done.1 = bf16[2,64,1024]{2,1,0:T(8,128)(2,1)} collective-permute-done((bf16[2,64,1024]{2,1,0:T(8,128)(2,1)}, bf16[2,64,1024]{2,1,0:T(8,128)(2,1)}, u32[]{:S(2)}, u32[]{:S(2)}) %collective-permute-start.1) | collective-permute-done | bytes 262176 | tf_op jit(solution)/shard_map/ppermute | solution.py:30
  40.6 1.2 collective-permute-start.3
  41.8 1.0 constant_dynamic-update-slice_fusion.5
  42.8 1.0 constant_dynamic-update-slice_fusion.4
  43.7 6.1 %collective-permute-done.3 = bf16[2,32,1024]{2,1,0:T(8,128)(2,1)S(1)} collective-permute-done((bf16[2,32,1024]{2,1,0:T(8,128)(2,1)S(1)}, bf16[2,32,1024]{2,1,0:T(8,128)(2,1)S(1)}, u32[]{:S(2)}, u32[]{:S(2)}) %collective-permute-start.3) | collective-permute-done | bytes 131104 | tf_op jit(solution)/shard_map/ppermute | solution.py:30
  49.9 0.9 constant_dynamic-update-slice_fusion.1
  50.8 0.9 constant_dynamic-update-slice_fusion.far_ref
  51.8 1.6 copy-done.6
  53.3 30.1 %forward_attention.1 = (bf16[8,4,896,256]{3,2,1,0:T(8,128)(2,1)}, bf16[1024,1024]{1,0:T(8,128)(2,1)S(1)}) custom-call(bf16[1024,1024]{1,0:T(8,128)(2,1)S(1)} %copy-done.6, bf16[1024,1024]{1,0:T(8,128)(2,1)S(1)} %copy-done, bf16[1024,1024]{1,0:T(8,128)(2,1)S(1)} %copy-done.2, bf16[2,384,1024]{2,1,0:T(8,128)(2,1)S(1)} %constant_dynamic-update-slice_fusion.far_ref, ...), custom_call_target="tpu_custom_call" | custom-call | flops 22548578304 | bytes 25165824 | tf_op jit(solution)/shard_map/forward_attention/pallas_call | solution.py:162
  83.4 6.0 %fusion.8 = bf16[1024,1024]{1,0:T(8,128)(2,1)} fusion(bf16[1024,1024]{1,0:T(8,128)(2,1)S(1)} %get-tuple-element.22, bf16[1024,4096]{1,0:T(8,128)(2,1)} %param.9, s32[]{:T(128)S(6)} %select_n.140), kind=kOutput, calls=%fused_computation.15 | convolution fusion | flops 2148532224 | bytes 6291460 | tf_op jit(solution)/shard_map/dot_general | solution.py:25
  89.5 2.3 collective-permute-start.7
  91.8 5.3 %fusion.11 = bf16[1024,1024]{1,0:T(8,128)(2,1)} fusion(bf16[1024,1024]{1,0:T(8,128)(2,1)S(1)} %get-tuple-element.22, bf16[1024,4096]{1,0:T(8,128)(2,1)} %param.9, s32[]{:T(128)S(6)} %select_n.141), kind=kOutput, calls=%fused_computation.16 | convolution fusion | flops 2148532224 | bytes 6291460 | tf_op jit(solution)/shard_map/dot_general | solution.py:25
  97.0 0.5 collective-permute-start.8
  97.5 5.3 %fusion.14 = bf16[1024,1024]{1,0:T(8,128)(2,1)} fusion(bf16[1024,1024]{1,0:T(8,128)(2,1)S(1)} %get-tuple-element.22, bf16[1024,4096]{1,0:T(8,128)(2,1)} %param.9, s32[]{:T(128)S(6)} %select_n.142), kind=kOutput, calls=%fused_computation.17 | convolution fusion | flops 2148532224 | bytes 6291460 | tf_op jit(solution)/shard_map/dot_general | solution.py:25
  102.8 0.7 collective-permute-start.9
  103.5 48.4 %all-gather.2.cloned.1.call-done = bf16[1024,4096]{0,1:T(8,128)(2,1)} async-done(((bf16[1024,1024]{0,1:T(8,128)(2,1)}), bf16[1024,4096]{0,1:T(8,128)(2,1)}) %all-gather.2.cloned.1.call-update) | async-done | bytes 8388624 | tf_op jit(solution)/shard_map/all_gather | solution.py:133
  151.9 7.1 %constant_dynamic-slice_fusion.1 = (bf16[1024,4,1,512]{0,3,2,1:T(8,128)(2,1)}, bf16[1024,4,1,512]{0,3,2,1:T(8,128)(2,1)S(1)}) fusion(bf16[1024,4,2,512]{0,3,2,1:T(8,128)(2,1)} %bitcast.57, s32[]{:T(128)S(6)} %select_n.144, s32[]{:T(128)S(6)} %select_n.145), kind=kLoop, calls=%fused_computation.126 | loop fusion | bytes 16777224 | tf_op jit(solution)/shard_map/jit(dynamic_index_in_dim)/dynamic_slice | solution.py:204
  159.0 6.0 %convolution_convert_fusion = bf16[2048,1024]{1,0:T(8,128)(2,1)} fusion(bf16[1024,2048]{0,1:T(8,128)(2,1)S(1)} %bitcast.62, bf16[1024,1024]{1,0:T(8,128)(2,1)S(1)} %copy-done.9), kind=kOutput, calls=%fused_computation.4 | convolution fusion | flops 4297064448 | bytes 10485760 | tf_op jit(solution)/shard_map/dot_general | solution.py:25
  165.0 0.1 fusion.27
  165.4 26.0 %collective-permute-done.8 = bf16[1024,1024]{1,0:T(8,128)(2,1)} collective-permute-done((bf16[1024,1024]{1,0:T(8,128)(2,1)}, bf16[1024,1024]{1,0:T(8,128)(2,1)}, u32[]{:S(2)}, u32[]{:S(2)}) %collective-permute-start.8) | collective-permute-done | bytes 2097184 | tf_op jit(solution)/shard_map/ppermute | solution.py:30
  191.4 7.9 %add_convert_fusion.3 = bf16[1024,1024]{1,0:T(8,128)(2,1)} fusion(bf16[1024,1024]{1,0:T(8,128)(2,1)} %collective-permute-done.9, bf16[1024,1024]{1,0:T(8,128)(2,1)} %collective-permute-done.8, bf16[1024,1024]{1,0:T(8,128)(2,1)} %collective-permute-done.7, bf16[1024,1024]{1,0:T(8,128)(2,1)} %copy-done.8, bf16[1024,4096]{1,0:T(8,128)(2,1)} %param.9, ...), kind=kOutput, calls=%fused_computation.3 | convolution fusion | flops 2154823680 | bytes 12582916 | tf_op jit(solution)/shard_map/dot_general | solution.py:25
  199.3 12.8 %convolution_convert_fusion.1.g_ref = bf16[1024,1024]{1,0:T(8,128)(2,1)} fusion(bf16[1024,4096]{0,1:T(8,128)(2,1)S(1)} %bitcast.59, bf16[1024,4096]{1,0:T(8,128)(2,1)} %param.9), kind=kOutput, calls=%fused_computation.14 | convolution fusion | flops 8590983168 | bytes 18874368 | tf_op jit(solution)/shard_map/dot_general | solution.py:25
  212.1 6.3 %add_convert_fusion = bf16[2048,1024]{1,0:T(8,128)(2,1)S(1)} fusion(bf16[2048,1024]{1,0:T(8,128)(2,1)} %collective-permute-done.10, bf16[1024,2048]{0,1:T(8,128)(2,1)S(1)} %bitcast.61, bf16[1024,1024]{1,0:T(8,128)(2,1)S(1)} %copy-done.10), kind=kOutput, calls=%fused_computation | convolution fusion | flops 4301258752 | bytes 14680064 | tf_op jit(solution)/shard_map/dot_general | solution.py:25
  218.4 0.5 dynamic-slice_bitcast_fusion
  218.9 1.6 collective-permute-start.11
  220.5 2.4 collective-permute-start.12
  222.9 0.5 collective-permute-start.13
  223.4 36.0 %backward_attention.1 = (bf16[1024,1024]{1,0:T(8,128)(2,1)}, f32[1024,1024]{1,0:T(8,128)}, f32[1024,1024]{1,0:T(8,128)}, bf16[2,384,1024]{2,1,0:T(8,128)(2,1)S(1)}) custom-call(bf16[1024,1024]{1,0:T(8,128)(2,1)S(1)} %copy-done.7, bf16[1024,1024]{1,0:T(8,128)(2,1)S(1)} %copy-done, bf16[1024,1024]{1,0:T(8,128)(2,1)S(1)} %copy-done.3, ...), custom_call_target="tpu_custom_call" | custom-call | flops 30064771072 | bytes 37748736 | tf_op jit(solution)/shard_map/backward_attention/pallas_call | solution.py:219
  259.4 6.1 %collective-permute-done.11 = bf16[512,1024]{1,0:T(8,128)(2,1)S(1)} collective-permute-done((bf16[512,1024]{1,0:T(8,128)(2,1)S(1)}, bf16[512,1024]{1,0:T(8,128)(2,1)S(1)}, u32[]{:S(2)}, u32[]{:S(2)}) %collective-permute-start.11) | collective-permute-done | bytes 1048608 | tf_op jit(solution)/shard_map/ppermute | solution.py:30
  265.5 26.9 %collective-permute-done.12 = bf16[512,1024]{1,0:T(8,128)(2,1)S(1)} collective-permute-done((bf16[512,1024]{1,0:T(8,128)(2,1)S(1)}, bf16[512,1024]{1,0:T(8,128)(2,1)S(1)}, u32[]{:S(2)}, u32[]{:S(2)}) %collective-permute-start.12) | collective-permute-done | bytes 1048608 | tf_op jit(solution)/shard_map/ppermute | solution.py:30
  292.5 0.1 collective-permute-start.20
  292.6 2.5 collective-permute-start.19
  295.0 1.2 collective-permute-start.14
  296.2 25.3 %collective-permute-start.16 = (bf16[2,64,1024]{2,1,0:T(8,128)(2,1)S(1)}, bf16[2,64,1024]{2,1,0:T(8,128)(2,1)S(1)}, u32[]{:S(2)}, u32[]{:S(2)}) collective-permute-start(bf16[2,64,1024]{2,1,0:T(8,128)(2,1)S(1)} %get-tuple-element.49), channel_id=1, source_target_pairs={{0,12},{4,8},{8,4},{12,0},{16,28},{20,24},{24,20},{28,16},{1,13},{... | collective-permute-start | bytes 786440 | tf_op jit(solution)/shard_map/ppermute | solution.py:30
  321.5 0.4 collective-permute-start.15
  321.9 2.2 convert_add_fusion
  324.1 2.2 collective-permute-start.18
  326.3 10.5 %collective-permute-done.15 = bf16[2,64,1024]{2,1,0:T(8,128)(2,1)S(1)} collective-permute-done((bf16[2,64,1024]{2,1,0:T(8,128)(2,1)S(1)}, bf16[2,64,1024]{2,1,0:T(8,128)(2,1)S(1)}, u32[]{:S(2)}, u32[]{:S(2)}) %collective-permute-start.15) | collective-permute-done | bytes 262176 | tf_op jit(solution)/shard_map/ppermute | solution.py:30
  336.8 0.3 collective-permute-start.17
  337.2 7.8 %collective-permute-done.17 = bf16[2,32,1024]{2,1,0:T(8,128)(2,1)S(1)} collective-permute-done((bf16[2,32,1024]{2,1,0:T(8,128)(2,1)S(1)}, bf16[2,32,1024]{2,1,0:T(8,128)(2,1)S(1)}, u32[]{:S(2)}, u32[]{:S(2)}) %collective-permute-start.17) | collective-permute-done | bytes 131104 | tf_op jit(solution)/shard_map/ppermute | solution.py:30
  345.0 1.3 fusion.25
  346.4 1.3 fusion.26
  347.7 0.9 copy-done.12
  348.6 2.1 add_convert_fusion.1
  350.6 0.9 copy-done.11
  351.5 2.0 add_convert_fusion.2
  (101 shorter events, 0.9 us)
Async XLA Ops:
  7.2 144.7 %all-gather.2.cloned.1.call-start = ((), (), s32[]{:S(2)}) async-start(), calls=%async_computation | async-start | bytes 10485760 | tf_op jit(solution)/shard_map/all_gather | solution.py:133
  11.2 2.3 copy-start
  11.2 8.4 %copy-start.14 = (pred[1024]{0:T(1024)(128)(4,1)}, pred[1024]{0:T(1024)(128)(4,1)S(1)}, u32[]{:S(2)}) copy-start(pred[1024]{0:T(1024)(128)(4,1)S(1)} %get-tuple-element.54) | copy-start | bytes 3076
  11.2 7.9 %copy-start.1 = (bf16[1024,1024]{1,0:T(8,128)(2,1)S(1)}, bf16[1024,1024]{1,0:T(8,128)(2,1)}, u32[]{:S(2)}) copy-start(bf16[1024,1024]{1,0:T(8,128)(2,1)} %v_ref.3) | copy-start | bytes 6291460
  13.9 36.9 %collective-permute-start.6 = (bf16[2,32,1024]{2,1,0:T(8,128)(2,1)S(1)}, bf16[2,32,1024]{2,1,0:T(8,128)(2,1)}, u32[]{:S(2)}, u32[]{:S(2)}) collective-permute-start(bf16[2,32,1024]{2,1,0:T(8,128)(2,1)S(1)} %pad_maximum_fusion.2), channel_id=1, source_target_pairs={{0,28},{4,24},{8,20},{12,16},{16,12},{20,8},{24,4},{28,0},{1,29},{... | collective-permute-start | bytes 393224 | tf_op jit(solution)/shard_map/ppermute | solution.py:30
  18.5 31.4 %collective-permute-start.5 = (bf16[2,32,1024]{2,1,0:T(8,128)(2,1)S(1)}, bf16[2,32,1024]{2,1,0:T(8,128)(2,1)}, u32[]{:S(2)}, u32[]{:S(2)}) collective-permute-start(bf16[2,32,1024]{2,1,0:T(8,128)(2,1)S(1)} %pad_maximum_fusion.2), channel_id=1, source_target_pairs={{0,24},{4,28},{8,16},{12,20},{16,8},{20,12},{24,0},{28,4},{1,25},{... | collective-permute-start | bytes 393224 | tf_op jit(solution)/shard_map/ppermute | solution.py:30
  20.9 21.9 %collective-permute-start.2 = (bf16[2,64,1024]{2,1,0:T(8,128)(2,1)}, bf16[2,64,1024]{2,1,0:T(8,128)(2,1)}, u32[]{:S(2)}, u32[]{:S(2)}) collective-permute-start(bf16[2,64,1024]{2,1,0:T(8,128)(2,1)} %pad_maximum_fusion.1), channel_id=1, source_target_pairs={{0,12},{4,8},{8,4},{12,0},{16,28},{20,24},{24,20},{28,16},{1,13},{... | collective-permute-start | bytes 786440 | tf_op jit(solution)/shard_map/ppermute | solution.py:30
  20.9 19.8 %collective-permute-start.1 = (bf16[2,64,1024]{2,1,0:T(8,128)(2,1)}, bf16[2,64,1024]{2,1,0:T(8,128)(2,1)}, u32[]{:S(2)}, u32[]{:S(2)}) collective-permute-start(bf16[2,64,1024]{2,1,0:T(8,128)(2,1)} %pad_maximum_fusion.1), channel_id=1, source_target_pairs={{0,8},{4,12},{8,0},{12,4},{16,24},{20,28},{24,16},{28,20},{1,9},{5... | collective-permute-start | bytes 786440 | tf_op jit(solution)/shard_map/ppermute | solution.py:30
  22.5 1.0 copy-start.21
  22.5 1.0 copy-start.16
  22.6 1.0 copy-start.18
  23.0 0.9 copy-start.20
  23.6 2.0 collective-permute-start
  24.4 27.3 %copy-start.2 = (bf16[1024,1024]{1,0:T(8,128)(2,1)S(1)}, bf16[1024,1024]{1,0:T(8,128)(2,1)}, u32[]{:S(2)}) copy-start(bf16[1024,1024]{1,0:T(8,128)(2,1)} %v_ref.3) | copy-start | bytes 6291460
  25.6 24.3 %collective-permute-start.4 = (bf16[2,32,1024]{2,1,0:T(8,128)(2,1)S(1)}, bf16[2,32,1024]{2,1,0:T(8,128)(2,1)S(1)}, u32[]{:S(2)}, u32[]{:S(2)}) collective-permute-start(bf16[2,32,1024]{2,1,0:T(8,128)(2,1)S(1)} %pad_maximum_fusion.2), channel_id=1, source_target_pairs={{0,20},{4,16},{8,28},{12,24},{16,4},{20,0},{24,12},{28,8},{1,21},{... | collective-permute-start | bytes 393224 | tf_op jit(solution)/shard_map/ppermute | solution.py:30
  40.6 9.2 %collective-permute-start.3 = (bf16[2,32,1024]{2,1,0:T(8,128)(2,1)S(1)}, bf16[2,32,1024]{2,1,0:T(8,128)(2,1)S(1)}, u32[]{:S(2)}, u32[]{:S(2)}) collective-permute-start(bf16[2,32,1024]{2,1,0:T(8,128)(2,1)S(1)} %pad_maximum_fusion.2), channel_id=1, source_target_pairs={{0,16},{4,20},{8,24},{12,28},{16,0},{20,4},{24,8},{28,12},{1,17},{... | collective-permute-start | bytes 393224 | tf_op jit(solution)/shard_map/ppermute | solution.py:30
  51.7 1.6 copy-start.6
  53.3 30.1 %copy-start.4 = (bf16[2,384,1024]{2,1,0:T(8,128)(2,1)}, bf16[2,384,1024]{2,1,0:T(8,128)(2,1)S(1)}, u32[]{:S(2)}) copy-start(bf16[2,384,1024]{2,1,0:T(8,128)(2,1)S(1)} %constant_dynamic-update-slice_fusion.far_ref) | copy-start | bytes 4718596
  83.4 14.1 %copy-start.8 = (bf16[1024,1024]{1,0:T(8,128)(2,1)}, bf16[1024,1024]{1,0:T(8,128)(2,1)S(1)}, u32[]{:S(2)}) copy-start(bf16[1024,1024]{1,0:T(8,128)(2,1)S(1)} %get-tuple-element.22) | copy-start | bytes 6291460
  89.5 75.9 %collective-permute-start.7 = (bf16[1024,1024]{1,0:T(8,128)(2,1)}, bf16[1024,1024]{1,0:T(8,128)(2,1)}, u32[]{:S(2)}, u32[]{:S(2)}) collective-permute-start(bf16[1024,1024]{1,0:T(8,128)(2,1)} %fusion.8), channel_id=1, source_target_pairs={{0,3},{1,2},{2,1},{3,0},{4,7},{5,6},{6,5},{7,4},{8,11},{9,10},{10,... | collective-permute-start | bytes 6291464 | tf_op jit(solution)/shard_map/ppermute | solution.py:30
  97.0 94.3 %collective-permute-start.8 = (bf16[1024,1024]{1,0:T(8,128)(2,1)}, bf16[1024,1024]{1,0:T(8,128)(2,1)}, u32[]{:S(2)}, u32[]{:S(2)}) collective-permute-start(bf16[1024,1024]{1,0:T(8,128)(2,1)} %fusion.11), channel_id=1, source_target_pairs={{0,2},{1,3},{2,0},{3,1},{4,6},{5,7},{6,4},{7,5},{8,10},{9,11},{10,... | collective-permute-start | bytes 6291464 | tf_op jit(solution)/shard_map/ppermute | solution.py:30
  102.8 88.6 %collective-permute-start.9 = (bf16[1024,1024]{1,0:T(8,128)(2,1)}, bf16[1024,1024]{1,0:T(8,128)(2,1)}, u32[]{:S(2)}, u32[]{:S(2)}) collective-permute-start(bf16[1024,1024]{1,0:T(8,128)(2,1)} %fusion.14), channel_id=1, source_target_pairs={{0,1},{1,0},{2,3},{3,2},{4,5},{5,4},{6,7},{7,6},{8,9},{9,8},{10,11... | collective-permute-start | bytes 6291464 | tf_op jit(solution)/shard_map/ppermute | solution.py:30
  151.9 7.1 %copy-start.9 = (bf16[1024,1024]{1,0:T(8,128)(2,1)S(1)}, bf16[1024,1024]{1,0:T(8,128)(2,1)}, u32[]{:S(2)}) copy-start(bf16[1024,1024]{1,0:T(8,128)(2,1)} %copy-done.8) | copy-start | bytes 6291460
  159.0 6.1 %copy-start.17 = (s32[1024]{0:T(1024)S(1)}, s32[1024]{0:T(1024)}, u32[]{:S(2)}) copy-start(s32[1024]{0:T(1024)} %copy-done.16) | copy-start | bytes 12292
  159.0 6.1 %copy-start.19 = (s32[1024]{0:T(1024)S(1)}, s32[1024]{0:T(1024)}, u32[]{:S(2)}) copy-start(s32[1024]{0:T(1024)} %copy-done.18) | copy-start | bytes 12292
  159.0 6.1 %copy-start.22 = (pred[1024]{0:T(1024)(128)(4,1)S(1)}, pred[1024]{0:T(1024)(128)(4,1)}, u32[]{:S(2)}) copy-start(pred[1024]{0:T(1024)(128)(4,1)} %copy-done.21) | copy-start | bytes 3076
  159.0 6.1 %copy-start.15 = (pred[1024]{0:T(1024)(128)(4,1)S(1)}, pred[1024]{0:T(1024)(128)(4,1)}, u32[]{:S(2)}) copy-start(pred[1024]{0:T(1024)(128)(4,1)} %copy-done.14) | copy-start | bytes 3076
  165.0 47.1 %collective-permute-start.10 = (bf16[2048,1024]{1,0:T(8,128)(2,1)}, bf16[2048,1024]{1,0:T(8,128)(2,1)}, u32[]{:S(2)}, u32[]{:S(2)}) collective-permute-start(bf16[2048,1024]{1,0:T(8,128)(2,1)} %convolution_convert_fusion), channel_id=1, source_target_pairs={{0,4},{4,0},{8,12},{12,8},{16,20},{20,16},{24,28},{28,24},{1,5},{5... | collective-permute-start | bytes 12582920 | tf_op jit(solution)/shard_map/ppermute | solution.py:30
  165.3 34.0 %slice-start = ((s8[8388608]{0:T(1024)(128)(4,1)}), s8[4194304]{0:T(1024)(128)(4,1)S(1)}, s32[]{:S(2)}) async-start(s8[8388608]{0:T(1024)(128)(4,1)} %bitcast.58), calls=%async_computation.1 | async-start | bytes 8388608
  165.3 33.9 %slice-start.1 = ((s8[8388608]{0:T(1024)(128)(4,1)}), s8[4194304]{0:T(1024)(128)(4,1)S(1)}, s32[]{:S(2)}) async-start(s8[8388608]{0:T(1024)(128)(4,1)} %bitcast.58), calls=%async_computation.2 | async-start | bytes 8388608
  199.3 12.8 %copy-start.10 = (bf16[1024,1024]{1,0:T(8,128)(2,1)S(1)}, bf16[1024,1024]{1,0:T(8,128)(2,1)}, u32[]{:S(2)}) copy-start(bf16[1024,1024]{1,0:T(8,128)(2,1)} %copy-done.8) | copy-start | bytes 6291460
  199.3 12.8 %copy-start.13 = (bf16[1024,4,1,512]{0,3,2,1:T(8,128)(2,1)S(1)}, bf16[1024,4,1,512]{0,3,2,1:T(8,128)(2,1)}, u32[]{:S(2)}) copy-start(bf16[1024,4,1,512]{0,3,2,1:T(8,128)(2,1)} %get-tuple-element.39) | copy-start | bytes 12582916
  218.4 5.0 %copy-start.3 = (bf16[1024,1024]{1,0:T(8,128)(2,1)S(1)}, bf16[1024,1024]{1,0:T(8,128)(2,1)}, u32[]{:S(2)}) copy-start(bf16[1024,1024]{1,0:T(8,128)(2,1)} %v_ref.3) | copy-start | bytes 6291460
  218.4 4.9 %copy-start.5 = (bf16[2,384,1024]{2,1,0:T(8,128)(2,1)S(1)}, bf16[2,384,1024]{2,1,0:T(8,128)(2,1)}, u32[]{:S(2)}) copy-start(bf16[2,384,1024]{2,1,0:T(8,128)(2,1)} %copy-done.4) | copy-start | bytes 4718596
  218.4 4.9 %copy-start.7 = (bf16[1024,1024]{1,0:T(8,128)(2,1)S(1)}, bf16[1024,1024]{1,0:T(8,128)(2,1)}, u32[]{:S(2)}) copy-start(bf16[1024,1024]{1,0:T(8,128)(2,1)} %q_ref.3) | copy-start | bytes 6291460
  218.9 46.6 %collective-permute-start.11 = (bf16[512,1024]{1,0:T(8,128)(2,1)S(1)}, bf16[512,1024]{1,0:T(8,128)(2,1)S(1)}, u32[]{:S(2)}, u32[]{:S(2)}) collective-permute-start(bf16[512,1024]{1,0:T(8,128)(2,1)S(1)} %get-tuple-element.29), channel_id=1, source_target_pairs={{0,8},{4,12},{8,0},{12,4},{16,24},{20,28},{24,16},{28,20},{1,9},{5... | collective-permute-start | bytes 3145736 | tf_op jit(solution)/shard_map/ppermute | solution.py:30
  220.5 71.9 %collective-permute-start.12 = (bf16[512,1024]{1,0:T(8,128)(2,1)S(1)}, bf16[512,1024]{1,0:T(8,128)(2,1)S(1)}, u32[]{:S(2)}, u32[]{:S(2)}) collective-permute-start(bf16[512,1024]{1,0:T(8,128)(2,1)S(1)} %get-tuple-element.30), channel_id=1, source_target_pairs={{0,16},{4,20},{8,24},{12,28},{16,0},{20,4},{24,8},{28,12},{1,17},{... | collective-permute-start | bytes 3145736 | tf_op jit(solution)/shard_map/ppermute | solution.py:30
  222.9 69.5 %collective-permute-start.13 = (bf16[512,1024]{1,0:T(8,128)(2,1)S(1)}, bf16[512,1024]{1,0:T(8,128)(2,1)S(1)}, u32[]{:S(2)}, u32[]{:S(2)}) collective-permute-start(bf16[512,1024]{1,0:T(8,128)(2,1)S(1)} %get-tuple-element.31), channel_id=1, source_target_pairs={{0,24},{4,28},{8,16},{12,20},{16,8},{20,12},{24,0},{28,4},{1,25},{... | collective-permute-start | bytes 3145736 | tf_op jit(solution)/shard_map/ppermute | solution.py:30
  292.5 52.5 %collective-permute-start.20 = (bf16[2,32,1024]{2,1,0:T(8,128)(2,1)S(1)}, bf16[2,32,1024]{2,1,0:T(8,128)(2,1)S(1)}, u32[]{:S(2)}, u32[]{:S(2)}) collective-permute-start(bf16[2,32,1024]{2,1,0:T(8,128)(2,1)S(1)} %get-tuple-element.45), channel_id=1, source_target_pairs={{0,28},{4,24},{8,20},{12,16},{16,12},{20,8},{24,4},{28,0},{1,29},{... | collective-permute-start | bytes 393224 | tf_op jit(solution)/shard_map/ppermute | solution.py:30
  292.6 52.4 %collective-permute-start.19 = (bf16[2,32,1024]{2,1,0:T(8,128)(2,1)S(1)}, bf16[2,32,1024]{2,1,0:T(8,128)(2,1)S(1)}, u32[]{:S(2)}, u32[]{:S(2)}) collective-permute-start(bf16[2,32,1024]{2,1,0:T(8,128)(2,1)S(1)} %get-tuple-element.46), channel_id=1, source_target_pairs={{0,24},{4,28},{8,16},{12,20},{16,8},{20,12},{24,0},{28,4},{1,25},{... | collective-permute-start | bytes 393224 | tf_op jit(solution)/shard_map/ppermute | solution.py:30
  295.0 29.1 %collective-permute-start.14 = (bf16[2,128,1024]{2,1,0:T(8,128)(2,1)S(1)}, bf16[2,128,1024]{2,1,0:T(8,128)(2,1)S(1)}, u32[]{:S(2)}, u32[]{:S(2)}) collective-permute-start(bf16[2,128,1024]{2,1,0:T(8,128)(2,1)S(1)} %slice.39), channel_id=1, source_target_pairs={{0,4},{4,0},{8,12},{12,8},{16,20},{20,16},{24,28},{28,24},{1,5},{5... | collective-permute-start | bytes 1572872 | tf_op jit(solution)/shard_map/ppermute | solution.py:30
  296.2 40.9 %collective-permute-start.16 = (bf16[2,64,1024]{2,1,0:T(8,128)(2,1)S(1)}, bf16[2,64,1024]{2,1,0:T(8,128)(2,1)S(1)}, u32[]{:S(2)}, u32[]{:S(2)}) collective-permute-start(bf16[2,64,1024]{2,1,0:T(8,128)(2,1)S(1)} %get-tuple-element.49), channel_id=1, source_target_pairs={{0,12},{4,8},{8,4},{12,0},{16,28},{20,24},{24,20},{28,16},{1,13},{... | collective-permute-start | bytes 786440 | tf_op jit(solution)/shard_map/ppermute | solution.py:30
  321.5 15.3 %collective-permute-start.15 = (bf16[2,64,1024]{2,1,0:T(8,128)(2,1)S(1)}, bf16[2,64,1024]{2,1,0:T(8,128)(2,1)S(1)}, u32[]{:S(2)}, u32[]{:S(2)}) collective-permute-start(bf16[2,64,1024]{2,1,0:T(8,128)(2,1)S(1)} %get-tuple-element.50), channel_id=1, source_target_pairs={{0,8},{4,12},{8,0},{12,4},{16,24},{20,28},{24,16},{28,20},{1,9},{5... | collective-permute-start | bytes 786440 | tf_op jit(solution)/shard_map/ppermute | solution.py:30
  324.1 20.9 %collective-permute-start.18 = (bf16[2,32,1024]{2,1,0:T(8,128)(2,1)S(1)}, bf16[2,32,1024]{2,1,0:T(8,128)(2,1)S(1)}, u32[]{:S(2)}, u32[]{:S(2)}) collective-permute-start(bf16[2,32,1024]{2,1,0:T(8,128)(2,1)S(1)} %get-tuple-element.47), channel_id=1, source_target_pairs={{0,20},{4,16},{8,28},{12,24},{16,4},{20,0},{24,12},{28,8},{1,21},{... | collective-permute-start | bytes 393224 | tf_op jit(solution)/shard_map/ppermute | solution.py:30
  336.8 8.1 %collective-permute-start.17 = (bf16[2,32,1024]{2,1,0:T(8,128)(2,1)S(1)}, bf16[2,32,1024]{2,1,0:T(8,128)(2,1)S(1)}, u32[]{:S(2)}, u32[]{:S(2)}) collective-permute-start(bf16[2,32,1024]{2,1,0:T(8,128)(2,1)S(1)} %get-tuple-element.48), channel_id=1, source_target_pairs={{0,16},{4,20},{8,24},{12,28},{16,0},{20,4},{24,8},{28,12},{1,17},{... | collective-permute-start | bytes 393224 | tf_op jit(solution)/shard_map/ppermute | solution.py:30
  346.4 2.2 copy-start.12
  348.6 2.9 copy-start.11
Sparse Core Ops, SparseCore 0:
  11.3 140.5 all-gather.1

commit v2 on v1

--- a/solution.py
+++ b/solution.py
@@ -112,6 +112,57 @@
             )
 
 
+def exchange_kernel(messages, source_ref, target_ref, send_sem, recv_sem):
+    me = lax.axis_index("seq")
+    peers = []
+    for mask, _, _, _ in messages:
+        peer, bit = me, 1
+        while bit <= mask:
+            if mask & bit:
+                peer = peer + bit - 2 * bit * ((me // bit) % 2)
+            bit *= 2
+        peers.append(peer)
+    barrier = pltpu.get_barrier_semaphore()
+    for peer in peers:
+        pl.semaphore_signal(
+            barrier, inc=1, device_id={"seq": peer}, device_id_type=pl.DeviceIdType.MESH
+        )
+    pl.semaphore_wait(barrier, len(peers))
+    copies = []
+    for slot in reversed(range(len(messages))):
+        _, source_at, target_at, count = messages[slot]
+        copy = pltpu.make_async_remote_copy(
+            src_ref=source_ref.at[:, pl.ds(source_at, count)],
+            dst_ref=target_ref.at[:, pl.ds(target_at, count)],
+            send_sem=send_sem.at[slot],
+            recv_sem=recv_sem.at[slot],
+            device_id={"seq": peers[slot]},
+            device_id_type=pl.DeviceIdType.MESH,
+        )
+        copy.start()
+        copies.append(copy)
+    for copy in copies:
+        copy.wait()
+
+
+def exchange(source, messages, rows, ident):
+    return pl.pallas_call(
+        functools.partial(exchange_kernel, messages),
+        out_shape=jax.ShapeDtypeStruct((2, rows, source.shape[2]), source.dtype),
+        in_specs=[pl.BlockSpec(memory_space=pltpu.VMEM)],
+        out_specs=pl.BlockSpec(memory_space=pltpu.VMEM),
+        scratch_shapes=[
+            pltpu.SemaphoreType.DMA((len(messages),)),
+            pltpu.SemaphoreType.DMA((len(messages),)),
+        ],
+        compiler_params=pltpu.CompilerParams(
+            collective_id=ident, has_side_effects=True, vmem_limit_bytes=16 * 1024 * 1024
+        ),
+        cost_estimate=pl.CostEstimate(flops=0, bytes_accessed=40 << 20, transcendentals=0),
+        name="exchange",
+    )(source)
+
+
 def body(queries, key_rows, value_rows, out_weight, cotangent, pattern):
     rows, features = queries.shape
     width = out_weight.shape[1]
@@ -126,21 +177,20 @@
     segments = keys_all // BLK
     where_seq = lax.axis_index("seq")
     where_head = lax.axis_index("head")
-    messages = [
-        (2**level + i, level, BLK >> level) for level in range(cross_levels) for i in range(2**level)
-    ]
-
-    grads_full = lax.all_gather(cotangent, "head", axis=1, tiled=True)
-
-    pools = [mean_matrix(BLK >> level, blocks << level) for level in range(cross_levels)]
-    far_own = []
-    for pool in pools:
-        far_own.append(
-            jnp.stack([dot(pool, key_rows), dot(pool, value_rows)]).astype(jnp.bfloat16)
-        )
-    far = jnp.concatenate(
-        [swapped(far_own[level], "seq", mask) for mask, level, _ in messages], axis=1
-    )
+    head_masks = [mask for mask in range(1, head_axis)]
+    chunks = [cotangent] + [swapped(cotangent, "head", mask) for mask in head_masks]
+
+    outward, homeward, pools, at = [], [], [], 0
+    for level in range(cross_levels):
+        count = BLK >> level
+        for i in range(2**level):
+            outward.append((2**level + i, sum(BLK >> below for below in range(level)), at, count))
+            homeward.append((2**level + i, at, at, count))
+            at += count
+        pools.append(mean_matrix(count, blocks << level))
+    pool_far = jnp.concatenate(pools, axis=0)
+    far_own = jnp.stack([dot(pool_far, key_rows), dot(pool_far, value_rows)]).astype(jnp.bfloat16)
+    far = exchange(far_own, outward, far_rows, 1)
 
     pool_two, pool_four = mean_matrix(BLK, 2), mean_matrix(BLK, 4)
     kept = jnp.where(
@@ -183,38 +233,46 @@
         name="forward_attention",
     )(queries, key_rows, value_rows, far, pool_two, pool_four, bias)
 
-    output = None
     share = width // head_axis
-    for mask in reversed(range(head_axis)):
-        target = where_head ^ mask
-        weight = lax.dynamic_slice_in_dim(out_weight, target * share, share, 1)
-        partial = dot(attended, weight)
-        if mask:
-            partial = swapped(partial.astype(jnp.bfloat16), "head", mask).astype(jnp.float32)
-        output = partial if output is None else output + partial
-    output = output.astype(jnp.bfloat16)
+    weights = [
+        lax.dynamic_slice_in_dim(out_weight, (where_head ^ mask) * share, share, 1)
+        for mask in range(head_axis)
+    ]
+    sums = [
+        swapped(dot(attended, weights[mask]).astype(jnp.bfloat16), "head", mask)
+        for mask in reversed(head_masks)
+    ]
+    own_sum = dot(attended, weights[0])
 
     core = where_seq & 1
     chip = where_seq >> 1
     chips = seq_count // 2
     piece = width // seq_count
-    by_core = grads_full.reshape(rows, chips, 2, piece)
+    groups = chips // head_axis
 
     def weight_grad(which):
-        chosen = lax.dynamic_index_in_dim(by_core, which, 2, keepdims=False)
-        return dot(chosen.reshape(rows, chips * piece), attended, TN)
+        chosen = [
+            lax.dynamic_index_in_dim(
+                chunk.reshape(rows, groups, 2, piece), which, 2, keepdims=False
+            ).reshape(rows, groups * piece)
+            for chunk in chunks
+        ]
+        return dot(jnp.concatenate(chosen, axis=1), attended, TN)
 
     theirs = swapped(weight_grad(1 - core).astype(jnp.bfloat16), "seq", 1)
-    mine = weight_grad(core)
-    grad_attn = dot(grads_full, out_weight, NT).astype(jnp.bfloat16)
-    theirs, grad_attn = lax.optimization_barrier((theirs, grad_attn))
-    mine = (mine + theirs.astype(jnp.float32)).astype(jnp.bfloat16)
+    mine = (weight_grad(core) + theirs.astype(jnp.float32)).astype(jnp.bfloat16)
     mine = mine.reshape(chips, piece, features)
-    parts = [
-        lax.dynamic_index_in_dim(mine, chip ^ mask, 0, keepdims=False) for mask in range(chips)
-    ]
-    parts, grad_attn = lax.optimization_barrier((parts, grad_attn))
+    parts = []
+    for mask in range(chips):
+        goal = chip ^ mask
+        spot = ((goal // groups) ^ where_head) * groups + goal % groups
+        parts.append(lax.dynamic_index_in_dim(mine, spot, 0, keepdims=False))
+    parts, chunks = lax.optimization_barrier((parts, chunks))
     arrived = [swapped(parts[mask], "seq", 2 * mask) for mask in range(1, chips)]
+
+    grad_attn = functools.reduce(
+        jnp.add, [dot(chunk, weight, NT) for chunk, weight in zip(chunks, weights)]
+    ).astype(jnp.bfloat16)
 
     grad_query, dk, dv, dfar = pl.pallas_call(
         backward_kernel,
@@ -234,16 +292,18 @@
         name="backward_attention",
     )(queries, key_rows, value_rows, grad_attn, far, pool_two, pool_four, prob)
 
-    arrived, dfar = lax.optimization_barrier((arrived, dfar))
+    arrived, sums, dfar = lax.optimization_barrier((arrived, sums, dfar))
     grad_weight = parts[0].astype(jnp.float32)
     for part in arrived:
         grad_weight = grad_weight + part.astype(jnp.float32)
-    returned, at = [], 0
-    for mask, level, count in messages:
-        returned.append(swapped(dfar[:, at : at + count], "seq", mask))
-        at += count
-    returned = jnp.concatenate(returned, axis=1)
-    spread = jnp.concatenate([pools[level] for _, level, _ in messages], axis=0)
+    output = own_sum
+    for part in sums:
+        output = output + part.astype(jnp.float32)
+    output = output.astype(jnp.bfloat16)
+    returned = exchange(dfar, homeward, far_rows, 2)
+    spread = jnp.concatenate(
+        [pool for level, pool in enumerate(pools) for _ in range(2**level)], axis=0
+    )
     grad_keys = (dk + dot(spread, returned[0], TN)).astype(jnp.bfloat16)
     grad_values = (dv + dot(spread, returned[1], TN)).astype(jnp.bfloat16)
     return (output, grad_query, grad_keys, grad_values, grad_weight)

time: 361 us -> 319 us (0.88); the launches traced: 360 us -> 313 us
  waiting for transfers between devices: 146 us -> 31.1 us
  Pallas kernels: 66.1 us -> 141 us
  starting transfers between devices: 50 us -> 12.4 us
  matrix products: 56.7 us -> 78 us
  local copies, waits for them, and re-layouts: 19.3 us -> 40.1 us
  between operations: 14.7 us -> 1.43 us
    pallas_call x0 -> x2, Pallas kernels: none -> 75.1 us  [exchange(): pl.pallas_call(functools.partial(exchange_kernel, messages), out_shape=ja...]
    ppermute x21 -> x10, waiting for transfers between devices: 97.7 us -> 31.1 us  [swapped(): return lax.ppermute(value, axis, pairs)]
    all_gather x1 -> x0, waiting for transfers between devices: 48.4 us -> none  [body(): grads_full = lax.all_gather(cotangent, 'head', axis=1, tiled=True)]
    ppermute x21 -> x10, starting transfers between devices: 50 us -> 12.4 us  [swapped(): return lax.ppermute(value, axis, pairs)]
    dot_general x15 -> x14, matrix products: 56.7 us -> 78 us  [dot(): lax.dot_general(left, right, dims, preferred_element_type=jnp.float32)]
    dynamic_slice x1 -> x11, local copies, waits for them, and re-layouts: 7.06 us -> 27.6 us  [weight_grad(): lax.dynamic_index_in_dim(chunk.reshape(rows, groups, 2, piece), which, 2,...]
    unnamed x64 -> x32, local copies, waits for them, and re-layouts: 10.4 us -> 11.8 us
  transfers between devices with their start and end apart: 22 -> 10, of which waited for: 9 -> 2; matrix products, arithmetic and copies ran while one was open for 17% -> 27% of each run, Pallas kernels for 18% -> 30%
where the time goes in v2:
time: 319 us; the launch traced here: 313 us
  Pallas kernels  141 us (44%)
  matrix products  78 us (24%)
  local copies, waits for them, and re-layouts  40.1 us (13%)
  waiting for transfers between devices  31.1 us (10%)
  starting transfers between devices  12.4 us (4%)
  other arithmetic  8.58 us (3%)
    dot_general x14, matrix products, dot(): lax.dot_general(left, right, dims, preferred_element_type=jnp.float32)  78 us
    pallas_call x2, Pallas kernels, exchange(): pl.pallas_call(functools.partial(exchange_kernel, messages), out_shape=ja...  75.1 us
    pallas_call x1, Pallas kernels, body(): pl.pallas_call(backward_kernel, grid=(heads,), out_shape=(jax.ShapeDtypeS...  35.9 us
    ppermute x10, waiting for transfers between devices, swapped(): return lax.ppermute(value, axis, pairs)  31.1 us
    pallas_call x1, Pallas kernels, body(): pl.pallas_call(forward_kernel, grid=(heads,), out_shape=(jax.ShapeDtypeSt...  30.1 us
    dynamic_slice x11, local copies, waits for them, and re-layouts, weight_grad(): lax.dynamic_index_in_dim(chunk.reshape(rows, groups, 2, piece), which, 2,...  27.6 us
    ppermute x10, starting transfers between devices, swapped(): return lax.ppermute(value, axis, pairs)  12.4 us
    unnamed x32, local copies, waits for them, and re-layouts  11.8 us
  transfers between devices with their start and end apart: 10, of which 2 were waited for; matrix products, arithmetic and copies ran while one was open for 27% of the time, Pallas kernels for 30%

profile of v2, /device:TPU:0, one launch (start us, length us, event | category | flops | bytes accessed | tf_op | source)
XLA Modules:
  0.0 312.6 jit_solution(6383653224138379833)
XLA Ops:
  0.6 0.0 copy-start.2
  0.7 4.1 %copy.22 = bf16[1024,1024]{0,1:T(8,128)(2,1)} copy(bf16[1024,1024]{1,0:T(8,128)(2,1)} %param.10) | data formatting | bytes 4194304 | tf_op args[4]
  4.7 3.9 %collective-permute-start.2 = (bf16[1024,1024]{0,1:T(8,128)(2,1)}, bf16[1024,1024]{0,1:T(8,128)(2,1)}, u32[]{:S(2)}, u32[]{:S(2)}) collective-permute-start(bf16[1024,1024]{0,1:T(8,128)(2,1)} %copy.22), channel_id=1, source_target_pairs={{0,3},{1,2},{2,1},{3,0},{4,7},{5,6},{6,5},{7,4},{8,11},{9,10},{10,... | collective-permute-start | bytes 6291464 | tf_op jit(solution)/shard_map/ppermute | solution.py:30
  8.6 0.5 collective-permute-start.1
  9.1 0.1 collective-permute-start
  9.3 0.1 slice_bitcast_fusion
  9.4 0.0 copy-start.5
  9.5 0.1 select_convert_fusion
  9.6 0.6 fusion.36
  10.2 0.8 copy-done.5
  11.0 0.6 fusion.37
  11.6 0.1 pad_maximum_fusion.source_ref
  11.7 28.2 %exchange.2.far_ref = bf16[2,384,1024]{2,1,0:T(8,128)(2,1)S(1)} custom-call(bf16[2,224,1024]{2,1,0:T(8,128)(2,1)S(1)} %pad_maximum_fusion.source_ref), custom_call_target="tpu_custom_call" | custom-call | bytes 41943040 | tf_op jit(solution)/shard_map/exchange/pallas_call | solution.py:149
  39.9 0.1 fusion.45
  40.0 0.1 copy.20
  40.1 0.1 broadcast_in_dim.63
  40.3 2.7 constant_dynamic-slice_fusion.7
  43.0 2.3 copy.30
  45.3 0.0 copy-start
  45.3 1.6 copy-done
  46.9 1.6 copy-done.3
  48.5 1.6 copy-done.6
  50.1 30.1 %forward_attention.1 = (bf16[8,4,896,256]{3,2,1,0:T(8,128)(2,1)}, bf16[1024,1024]{1,0:T(8,128)(2,1)S(1)}) custom-call(bf16[1024,1024]{1,0:T(8,128)(2,1)S(1)} %copy-done, bf16[1024,1024]{1,0:T(8,128)(2,1)S(1)} %copy-done.3, bf16[1024,1024]{1,0:T(8,128)(2,1)S(1)} %copy-done.6, bf16[2,384,1024]{2,1,0:T(8,128)(2,1)S(1)} %exchange.2.far_ref, ...), custom_call_target="tpu_custom_call" | custom-call | flops 22548578304 | bytes 25165824 | tf_op jit(solution)/shard_map/forward_attention/pallas_call | solution.py:212
  80.1 1.3 copy-done.8
  81.5 0.0 collective-permute-done.2
  81.5 18.1 %collective-permute-done.1 = bf16[1024,1024]{0,1:T(8,128)(2,1)} collective-permute-done((bf16[1024,1024]{0,1:T(8,128)(2,1)}, bf16[1024,1024]{0,1:T(8,128)(2,1)}, u32[]{:S(2)}, u32[]{:S(2)}) %collective-permute-start.1) | collective-permute-done | bytes 2097184 | tf_op jit(solution)/shard_map/ppermute | solution.py:30
  99.5 4.2 %constant_dynamic-slice_fusion.4 = (bf16[1024,1,1,512]{0,3,2,1:T(8,128)(2,1)}, bf16[1024,1,1,512]{0,3,2,1:T(8,128)(2,1)}, bf16[1024,1,1,512]{0,3,2,1:T(8,128)(2,1)}, bf16[1024,1,1,512]{0,3,2,1:T(8,128)(2,1)}) fusion(bf16[1024,1,2,512]{0,3,2,1:T(8,128)(2,1)} %bitcast.10, s32[]{:T(128)S(6)} %select_n.160, s32[]{:T(128)S(6)} %select_n.161, ...), kind=kLoop, calls=%fused_computation.104 | loop fusion | bytes 8388616 | tf_op jit(solution)/shard_map/jit(dynamic_index_in_dim)/dynamic_slice | solution.py:255
  103.8 2.3 copy.32
  106.0 2.3 copy.33
  108.3 3.0 constant_dynamic-slice_fusion.6
  111.3 2.4 copy.31
  113.8 9.5 %fusion.16 = bf16[2048,1024]{1,0:T(8,128)(2,1)} fusion(bf16[1024,1024]{1,0:T(8,128)(2,1)} %copy-done.8, bf16[1024,512]{1,0:T(8,128)(2,1)} %bitcast.59, bf16[1024,512]{1,0:T(8,128)(2,1)} %bitcast.58, bf16[1024,512]{1,0:T(8,128)(2,1)} %bitcast.63, bf16[1024,512]{1,0:T(8,128)(2,1)} %bitcast.57), kind=kOutput, calls=%fused_computation.21 | convolution fusion | flops 4313841664 | bytes 10485760 | tf_op jit(solution)/shard_map/dot_general | solution.py:25
  123.2 0.0 collective-permute-start.3
  123.2 5.9 %convolution_convert_fusion.2 = bf16[1024,1024]{1,0:T(8,128)(2,1)} fusion(bf16[1024,1024]{1,0:T(8,128)(2,1)} %copy-done.8, bf16[1024,4096]{1,0:T(8,128)(2,1)} %param.9, s32[]{:T(128)S(6)} %select_n.166), kind=kOutput, calls=%fused_computation.25 | convolution fusion | flops 2148532224 | bytes 6291460 | tf_op jit(solution)/shard_map/dot_general | solution.py:25
  129.1 1.7 collective-permute-start.7
  130.9 5.9 %convolution_convert_fusion.1 = bf16[1024,1024]{1,0:T(8,128)(2,1)} fusion(bf16[1024,1024]{1,0:T(8,128)(2,1)} %copy-done.8, bf16[1024,4096]{1,0:T(8,128)(2,1)} %param.9, s32[]{:T(128)S(6)} %select_n.167), kind=kOutput, calls=%fused_computation.24 | convolution fusion | flops 2148532224 | bytes 6291460 | tf_op jit(solution)/shard_map/dot_general | solution.py:25
  136.7 1.4 collective-permute-start.8
  138.1 5.9 %convolution_convert_fusion = bf16[1024,1024]{1,0:T(8,128)(2,1)} fusion(bf16[1024,1024]{1,0:T(8,128)(2,1)} %copy-done.8, bf16[1024,4096]{1,0:T(8,128)(2,1)} %param.9, s32[]{:T(128)S(6)} %select_n.168), kind=kOutput, calls=%fused_computation.23 | convolution fusion | flops 2148532224 | bytes 6291460 | tf_op jit(solution)/shard_map/dot_general | solution.py:25
  144.0 0.3 collective-permute-start.9
  144.4 1.3 copy.23
  145.7 0.1 constant_dynamic-update-slice_fusion.6
  145.9 6.5 %fusion.32 = f32[1024,1024]{1,0:T(8,128)} fusion(bf16[1024,1024]{1,0:T(8,128)(2,1)} %copy-done.8, bf16[1024,4096]{1,0:T(8,128)(2,1)} %param.9, s32[]{:T(128)S(6)} %select_n.159), kind=kOutput, calls=%fused_computation.37 | convolution fusion | flops 2147483648 | bytes 8388612 | tf_op jit(solution)/shard_map/dot_general | solution.py:25
  152.5 2.3 copy.29
  154.8 2.3 copy.27
  157.0 2.5 copy.25
  159.5 8.6 %add_convert_fusion = bf16[2048,1024]{1,0:T(8,128)(2,1)S(1)} fusion(bf16[2048,1024]{1,0:T(8,128)(2,1)} %collective-permute-done.3, bf16[1024,1024]{1,0:T(8,128)(2,1)} %copy-done.8, bf16[1024,512]{1,0:T(8,128)(2,1)} %bitcast.60, bf16[1024,512]{1,0:T(8,128)(2,1)} %bitcast.61, bf16[1024,512]{1,0:T(8,128)(2,1)} %bitcast.62, bf16[1024,512]{1,0:T(8,128)(2,1)} %bitcast.56), kind=kOutput, calls=%fused_computation | convolution fusion | flops 4318035968 | bytes 14680064 | tf_op jit(solution)/shard_map/dot_general | solution.py:25
  168.2 0.0 slice-start
  168.2 0.5 dynamic-slice_bitcast_fusion
  168.7 0.0 slice-start.1
  168.7 6.9 %fusion.21 = f32[1024,1024]{1,0:T(8,128)} fusion(bf16[1024,1024]{0,1:T(8,128)(2,1)} %collective-permute-done, bf16[1024,4096]{1,0:T(8,128)(2,1)} %param.9, s32[]{:T(128)S(6)} %select_n.168), kind=kOutput, calls=%fused_computation.26 | convolution fusion | flops 2147483648 | bytes 8388612 | tf_op jit(solution)/shard_map/dot_general | solution.py:25
  175.5 1.8 collective-permute-start.4
  177.3 2.6 collective-permute-start.5
  179.9 6.1 %fusion.24 = f32[1024,1024]{1,0:T(8,128)} fusion(bf16[1024,1024]{0,1:T(8,128)(2,1)} %collective-permute-done.1, bf16[1024,4096]{1,0:T(8,128)(2,1)S(1)} %bitcast.67, s32[]{:T(128)S(6)} %select_n.167), kind=kOutput, calls=%fused_computation.29 | convolution fusion | flops 2147483648 | bytes 8388612 | tf_op jit(solution)/shard_map/dot_general | solution.py:25
  186.0 4.4 %fusion.30 = f32[1024,1024]{1,0:T(8,128)} fusion(bf16[1024,1024]{1,0:T(8,128)(2,1)S(1)} %copy-done.11, bf16[1024,4096]{1,0:T(8,128)(2,1)S(1)} %bitcast.67, s32[]{:T(128)S(6)} %select_n.159), kind=kOutput, calls=%fused_computation.35 | convolution fusion | flops 2147483648 | bytes 8388612 | tf_op jit(solution)/shard_map/dot_general | solution.py:25
  190.4 9.5 %add_convert_fusion.4.g_ref = bf16[1024,1024]{1,0:T(8,128)(2,1)} fusion(f32[1024,1024]{1,0:T(8,128)} %fusion.24, f32[1024,1024]{1,0:T(8,128)} %fusion.30, f32[1024,1024]{1,0:T(8,128)} %fusion.21, bf16[1024,1024]{0,1:T(8,128)(2,1)} %collective-permute-done.2, bf16[1024,4096]{1,0:T(8,128)(2,1)S(1)} %bitcast.67, s32[]{:T(128)S(6)} %select_n.166), kind=kOutput, calls=%fused_computation.20 | convolution fusion | flops 2151677952 | bytes 18874372 | tf_op jit(solution)/shard_map/dot_general | solution.py:25
  199.9 0.1 collective-permute-start.6
  200.0 35.9 %backward_attention.1 = (bf16[1024,1024]{1,0:T(8,128)(2,1)}, f32[1024,1024]{1,0:T(8,128)}, f32[1024,1024]{1,0:T(8,128)}, bf16[2,384,1024]{2,1,0:T(8,128)(2,1)S(1)}) custom-call(bf16[1024,1024]{1,0:T(8,128)(2,1)S(1)} %copy-done.1, bf16[1024,1024]{1,0:T(8,128)(2,1)S(1)} %copy-done.4, bf16[1024,1024]{1,0:T(8,128)(2,1)S(1)} %copy-done.7, ...), custom_call_target="tpu_custom_call" | custom-call | flops 30064771072 | bytes 37748736 | tf_op jit(solution)/shard_map/backward_attention/pallas_call | solution.py:277
  235.9 13.0 %collective-permute-done.5 = bf16[512,1024]{1,0:T(8,128)(2,1)S(1)} collective-permute-done((bf16[512,1024]{1,0:T(8,128)(2,1)S(1)}, bf16[512,1024]{1,0:T(8,128)(2,1)S(1)}, u32[]{:S(2)}, u32[]{:S(2)}) %collective-permute-start.5) | collective-permute-done | bytes 1048608 | tf_op jit(solution)/shard_map/ppermute | solution.py:30
  248.9 46.9 %exchange.3 = bf16[2,384,1024]{2,1,0:T(8,128)(2,1)S(1)} custom-call(bf16[2,384,1024]{2,1,0:T(8,128)(2,1)S(1)} %get-tuple-element.41.source_ref), custom_call_target="tpu_custom_call" | custom-call | bytes 41943040 | tf_op jit(solution)/shard_map/exchange/pallas_call | solution.py:149
  295.9 5.0 %add_convert_fusion.1 = bf16[1024,1024]{1,0:T(8,128)(2,1)} fusion(f32[1024,1024]{1,0:T(8,128)} %get-tuple-element.42, bf16[384,1024]{1,0:T(8,128)(2,1)S(1)} %constant_dynamic-update-slice_fusion, bf16[2,384,1024]{2,1,0:T(8,128)(2,1)S(1)} %exchange.3), kind=kOutput, calls=%fused_computation.17 | convolution fusion | flops 807403520 | bytes 7864320 | tf_op jit(solution)/shard_map/dot_general | solution.py:25
  300.8 2.6 add_convert_fusion.2
  303.4 2.2 convert_add_fusion
  305.6 0.8 copy-done.9
  306.4 5.8 %add_convert_fusion.3 = bf16[1024,1024]{1,0:T(8,128)(2,1)} fusion(bf16[1024,1024]{1,0:T(8,128)(2,1)} %collective-permute-done.9, bf16[1024,1024]{1,0:T(8,128)(2,1)} %collective-permute-done.8, f32[1024,1024]{1,0:T(8,128)S(1)} %copy-done.9, bf16[1024,1024]{1,0:T(8,128)(2,1)} %collective-permute-done.7), kind=kLoop, calls=%fused_computation.19 | loop fusion | flops 7340032 | bytes 12582912 | tf_op jit(solution)/shard_map/convert_element_type | solution.py:302
  (50 shorter events, 0.4 us)
Async XLA Ops:
  0.6 8.6 %copy-start.12 = (s32[8,6]{1,0:T(8,128)S(1)}, s32[8,6]{1,0:T(8,128)}, u32[]{:S(2)}) copy-start(s32[8,6]{1,0:T(8,128)} %param.11) | copy-start | bytes 580
  0.6 8.9 %copy-start.2 = (bf16[1024,1024]{1,0:T(8,128)(2,1)S(1)}, bf16[1024,1024]{1,0:T(8,128)(2,1)}, u32[]{:S(2)}) copy-start(bf16[1024,1024]{1,0:T(8,128)(2,1)} %k_ref.3) | copy-start | bytes 6291460
  4.7 76.7 %collective-permute-start.2 = (bf16[1024,1024]{0,1:T(8,128)(2,1)}, bf16[1024,1024]{0,1:T(8,128)(2,1)}, u32[]{:S(2)}, u32[]{:S(2)}) collective-permute-start(bf16[1024,1024]{0,1:T(8,128)(2,1)} %copy.22), channel_id=1, source_target_pairs={{0,3},{1,2},{2,1},{3,0},{4,7},{5,6},{6,5},{7,4},{8,11},{9,10},{10,... | collective-permute-start | bytes 6291464 | tf_op jit(solution)/shard_map/ppermute | solution.py:30
  8.6 90.9 %collective-permute-start.1 = (bf16[1024,1024]{0,1:T(8,128)(2,1)}, bf16[1024,1024]{0,1:T(8,128)(2,1)}, u32[]{:S(2)}, u32[]{:S(2)}) collective-permute-start(bf16[1024,1024]{0,1:T(8,128)(2,1)} %copy.22), channel_id=1, source_target_pairs={{0,2},{1,3},{2,0},{3,1},{4,6},{5,7},{6,4},{7,5},{8,10},{9,11},{10,... | collective-permute-start | bytes 6291464 | tf_op jit(solution)/shard_map/ppermute | solution.py:30
  9.1 99.2 %collective-permute-start = (bf16[1024,1024]{0,1:T(8,128)(2,1)}, bf16[1024,1024]{0,1:T(8,128)(2,1)}, u32[]{:S(2)}, u32[]{:S(2)}) collective-permute-start(bf16[1024,1024]{0,1:T(8,128)(2,1)} %copy.22), channel_id=1, source_target_pairs={{0,1},{1,0},{2,3},{3,2},{4,5},{5,4},{6,7},{7,6},{8,9},{9,8},{10,11... | collective-permute-start | bytes 6291464 | tf_op jit(solution)/shard_map/ppermute | solution.py:30
  9.4 1.6 copy-start.5
  45.3 1.6 copy-start
  46.9 1.6 copy-start.3
  48.5 1.6 copy-start.6
  80.1 1.3 copy-start.8
  123.2 36.3 %collective-permute-start.3 = (bf16[2048,1024]{1,0:T(8,128)(2,1)}, bf16[2048,1024]{1,0:T(8,128)(2,1)}, u32[]{:S(2)}, u32[]{:S(2)}) collective-permute-start(bf16[2048,1024]{1,0:T(8,128)(2,1)} %fusion.16), channel_id=1, source_target_pairs={{0,4},{4,0},{8,12},{12,8},{16,20},{20,16},{24,28},{28,24},{1,5},{5... | collective-permute-start | bytes 12582920 | tf_op jit(solution)/shard_map/ppermute | solution.py:30
  129.1 70.8 %collective-permute-start.7 = (bf16[1024,1024]{1,0:T(8,128)(2,1)}, bf16[1024,1024]{1,0:T(8,128)(2,1)}, u32[]{:S(2)}, u32[]{:S(2)}) collective-permute-start(bf16[1024,1024]{1,0:T(8,128)(2,1)} %convolution_convert_fusion.2), channel_id=1, source_target_pairs={{0,3},{1,2},{2,1},{3,0},{4,7},{5,6},{6,5},{7,4},{8,11},{9,10},{10,... | collective-permute-start | bytes 6291464 | tf_op jit(solution)/shard_map/ppermute | solution.py:30
  136.7 99.2 %collective-permute-start.8 = (bf16[1024,1024]{1,0:T(8,128)(2,1)}, bf16[1024,1024]{1,0:T(8,128)(2,1)}, u32[]{:S(2)}, u32[]{:S(2)}) collective-permute-start(bf16[1024,1024]{1,0:T(8,128)(2,1)} %convolution_convert_fusion.1), channel_id=1, source_target_pairs={{0,2},{1,3},{2,0},{3,1},{4,6},{5,7},{6,4},{7,5},{8,10},{9,11},{10,... | collective-permute-start | bytes 6291464 | tf_op jit(solution)/shard_map/ppermute | solution.py:30
  144.0 91.9 %collective-permute-start.9 = (bf16[1024,1024]{1,0:T(8,128)(2,1)}, bf16[1024,1024]{1,0:T(8,128)(2,1)}, u32[]{:S(2)}, u32[]{:S(2)}) collective-permute-start(bf16[1024,1024]{1,0:T(8,128)(2,1)} %convolution_convert_fusion), channel_id=1, source_target_pairs={{0,1},{1,0},{2,3},{3,2},{4,5},{5,4},{6,7},{7,6},{8,9},{9,8},{10,11... | collective-permute-start | bytes 6291464 | tf_op jit(solution)/shard_map/ppermute | solution.py:30
  168.2 11.7 %slice-start = ((s8[8388608]{0:T(1024)(128)(4,1)}), s8[4194304]{0:T(1024)(128)(4,1)S(1)}, s32[]{:S(2)}) async-start(s8[8388608]{0:T(1024)(128)(4,1)} %bitcast.66), calls=%async_computation | async-start | bytes 8388608
  168.7 11.2 %slice-start.1 = ((s8[8388608]{0:T(1024)(128)(4,1)}), s8[4194304]{0:T(1024)(128)(4,1)S(1)}, s32[]{:S(2)}) async-start(s8[8388608]{0:T(1024)(128)(4,1)} %bitcast.66), calls=%async_computation.1 | async-start | bytes 8388608
  175.5 10.4 %copy-start.11 = (bf16[1024,1024]{1,0:T(8,128)(2,1)S(1)}, bf16[1024,1024]{1,0:T(8,128)(2,1)}, u32[]{:S(2)}) copy-start(bf16[1024,1024]{1,0:T(8,128)(2,1)} %param.10) | copy-start | bytes 6291460
  175.5 60.4 %collective-permute-start.4 = (bf16[512,1024]{1,0:T(8,128)(2,1)S(1)}, bf16[512,1024]{1,0:T(8,128)(2,1)S(1)}, u32[]{:S(2)}, u32[]{:S(2)}) collective-permute-start(bf16[512,1024]{1,0:T(8,128)(2,1)S(1)} %get-tuple-element.27), channel_id=1, source_target_pairs={{0,8},{4,12},{8,0},{12,4},{16,24},{20,28},{24,16},{28,20},{1,9},{5... | collective-permute-start | bytes 3145736 | tf_op jit(solution)/shard_map/ppermute | solution.py:30
  177.3 71.6 %collective-permute-start.5 = (bf16[512,1024]{1,0:T(8,128)(2,1)S(1)}, bf16[512,1024]{1,0:T(8,128)(2,1)S(1)}, u32[]{:S(2)}, u32[]{:S(2)}) collective-permute-start(bf16[512,1024]{1,0:T(8,128)(2,1)S(1)} %get-tuple-element.28), channel_id=1, source_target_pairs={{0,16},{4,20},{8,24},{12,28},{16,0},{20,4},{24,8},{28,12},{1,17},{... | collective-permute-start | bytes 3145736 | tf_op jit(solution)/shard_map/ppermute | solution.py:30
  190.4 9.6 %copy-start.1 = (bf16[1024,1024]{1,0:T(8,128)(2,1)S(1)}, bf16[1024,1024]{1,0:T(8,128)(2,1)}, u32[]{:S(2)}) copy-start(bf16[1024,1024]{1,0:T(8,128)(2,1)} %q_ref.3) | copy-start | bytes 6291460
  190.4 9.6 %copy-start.4 = (bf16[1024,1024]{1,0:T(8,128)(2,1)S(1)}, bf16[1024,1024]{1,0:T(8,128)(2,1)}, u32[]{:S(2)}) copy-start(bf16[1024,1024]{1,0:T(8,128)(2,1)} %k_ref.3) | copy-start | bytes 6291460
  190.4 9.6 %copy-start.7 = (bf16[1024,1024]{1,0:T(8,128)(2,1)S(1)}, bf16[1024,1024]{1,0:T(8,128)(2,1)}, u32[]{:S(2)}) copy-start(bf16[1024,1024]{1,0:T(8,128)(2,1)} %v_ref.3) | copy-start | bytes 6291460
  199.9 49.0 %collective-permute-start.6 = (bf16[512,1024]{1,0:T(8,128)(2,1)S(1)}, bf16[512,1024]{1,0:T(8,128)(2,1)S(1)}, u32[]{:S(2)}, u32[]{:S(2)}) collective-permute-start(bf16[512,1024]{1,0:T(8,128)(2,1)S(1)} %get-tuple-element.29), channel_id=1, source_target_pairs={{0,24},{4,28},{8,16},{12,20},{16,8},{20,12},{24,0},{28,4},{1,25},{... | collective-permute-start | bytes 3145736 | tf_op jit(solution)/shard_map/ppermute | solution.py:30
  295.8 5.0 %copy-start.10 = (f32[1024,1024]{1,0:T(8,128)S(1)}, f32[1024,1024]{1,0:T(8,128)}, u32[]{:S(2)}) copy-start(f32[1024,1024]{1,0:T(8,128)} %get-tuple-element.40) | copy-start | bytes 12582916
  303.4 2.9 copy-start.9
